TPU v7x, 256 devices: a whole 4x4x8 slice. The times are simulated.
256 devices in a mesh: grp: 32 (over z_hi, x, core), mem: 8 (over z_lo, y).
Axes of the slice: x: 4, y: 4, z: 8 (z_hi: 4, z_lo: 2; z = z_hi * 2 + z_lo), core: 2. Of those that a mesh axis runs over, the one named last changes fastest.
Arguments:
- picture_vectors: bfloat16 [16384, 1152], P(('grp', 'mem')), may hold values from -1.0234375 to 1.0234375
- caption_vectors: bfloat16 [16384, 1152], P(('grp', 'mem')), may hold values from -1.0234375 to 1.0234375
- matching_caption_position: int32 [16384], P('grp'), may hold values from 0 to 16383, each once
- learned_warmth_exponent: float32 [1], replicated, may hold values from 0.5 to 1.5
- offset_term: float32 [1], replicated, may hold values from -6 to -2
Outputs:
- image_grad: float32 [16384, 1152], P(('grp', 'mem'))
- text_grad: float32 [16384, 1152], P(('grp', 'mem'))
- statistics: float32 [3], replicated
Inputs may be any that keep to these rules, and one draw needn't show every extreme that they name: `matching_caption_position`: it is a permutation of the text rows: every text row is the positive of exactly one image row.
All inputs are finite; a program needn't handle non-finite values.
Results may differ from a plain program's by a relative error of at most 0.0011.
Values may be sent and summed in bfloat16 or wider, within the bound.
A program may use at most 64 MiB of HBM per device.

v0:
```python
import jax
import jax.numpy as jnp
from jax import lax
from jax.sharding import PartitionSpec as P


def score_tile(
    images_in_group,
    labels_in_group,
    segment_part,
    rows_per_member,
    member_count,
    member_index,
    warmth_factor,
    offset_value,
):
    local_index = jnp.arange(segment_part.shape[0], dtype=jnp.int32)
    columns = (
        local_index // rows_per_member * member_count + member_index
    ) * rows_per_member + local_index % rows_per_member
    affinity_matrix = lax.dot_general(
        images_in_group, segment_part, (((1,), (1,)), ((), ())), preferred_element_type=jnp.float32
    )
    matched_affinity = warmth_factor * affinity_matrix + offset_value
    label_sign = jnp.where(labels_in_group[:, None] == columns[None, :], 1.0, -1.0).astype(
        jnp.float32
    )
    accumulated_objective = -jnp.sum(jax.nn.log_sigmoid(label_sign * matched_affinity))
    derivative_factor = -label_sign * jax.nn.sigmoid(-label_sign * matched_affinity)
    sufficient_quantities = jnp.stack(
        [
            accumulated_objective,
            jnp.sum(derivative_factor * warmth_factor * affinity_matrix),
            jnp.sum(derivative_factor),
        ]
    )
    return (derivative_factor.astype(jnp.bfloat16), sufficient_quantities)


def on_device(
    picture_vectors,
    caption_vectors,
    matching_caption_position,
    learned_warmth_exponent,
    offset_term,
):
    warmth_factor = jnp.exp(learned_warmth_exponent[0])
    offset_value = offset_term[0]
    rows_per_member = picture_vectors.shape[0]
    member_count = lax.axis_size("mem")
    grp_count = lax.axis_size("grp")
    member_index = lax.axis_index("mem")
    matched_number = rows_per_member * member_count * grp_count
    images_in_group = lax.all_gather(picture_vectors, "mem", axis=0, tiled=True)
    segment_part = lax.all_gather(caption_vectors, "grp", axis=0, tiled=True)
    coef_half, sufficient_quantities = score_tile(
        images_in_group,
        matching_caption_position,
        segment_part,
        rows_per_member,
        member_count,
        member_index,
        warmth_factor,
        offset_value,
    )
    image_acc = jnp.dot(coef_half, segment_part, preferred_element_type=jnp.float32)
    text_part = lax.dot_general(
        coef_half, images_in_group, (((0,), (0,)), ((), ())), preferred_element_type=jnp.float32
    )
    text_acc = text_part
    image_acc, text_acc, stat_sums = (image_acc, text_acc, sufficient_quantities)
    text_total = lax.psum_scatter(text_acc, "grp", scatter_dimension=0, tiled=True)
    image_total = lax.psum_scatter(image_acc, "mem", scatter_dimension=0, tiled=True)
    totals = lax.psum(stat_sums, ("grp", "mem"))
    stretch_factor = warmth_factor / matched_number
    image_grad = image_total * stretch_factor
    text_grad = text_total * stretch_factor
    statistics = totals / float(matched_number * matched_number)
    return (image_grad, text_grad, statistics)


def solution(mesh):
    in_specs = (P(("grp", "mem"), None), P(("grp", "mem"), None), P("grp"), P(), P())
    out_specs = (P(("grp", "mem"), None), P(("grp", "mem"), None), P())
    return jax.shard_map(
        on_device, mesh=mesh, in_specs=in_specs, out_specs=out_specs, check_vma=False
    )
```

profile of v0, /device:TPU:1, one launch (start us, length us, event | category | flops | bytes accessed | tf_op | source)
XLA Modules:
  0.0 318.5 jit_solution(18254471438255421419)
XLA Ops:
  7.2 0.0 all-gather.3.cloned.1.call-start
  7.2 0.7 all-gather.3.cloned.1.call-update
  7.9 0.0 all-gather.5.cloned.1.call-start
  7.9 0.7 all-gather.5.cloned.1.call-update
  8.6 0.0 reduce-scatter.3.cloned.1.call-start
  10.0 40.6 %all-gather.3.cloned.1.call-done = bf16[512,1152]{1,0:T(8,128)(2,1)} async-done(((bf16[64,1152]{1,0:T(8,128)(2,1)}), bf16[512,1152]{1,0:T(8,128)(2,1)}) %all-gather.3.cloned.1.call-update) | async-done | bytes 1179664 | tf_op jit(solution)/shard_map/all_gather | solution.py:54
  50.7 69.4 %all-gather.5.cloned.1.call-done = bf16[2048,1152]{1,0:T(8,128)(2,1)} async-done(((bf16[64,1152]{1,0:T(8,128)(2,1)}), bf16[2048,1152]{1,0:T(8,128)(2,1)}) %all-gather.5.cloned.1.call-update) | async-done | bytes 4718608 | tf_op jit(solution)/shard_map/all_gather | solution.py:55
  120.1 0.0 copy-start
  120.1 0.0 copy-start.2
  120.1 10.1 %fusion.7 = (f32[]{:T(128)}, f32[]{:T(128)}, f32[]{:T(128)}, f32[512,2048]{1,0:T(8,128)S(1)}) fusion(f32[]{:T(128)} %bitcast.10, f32[]{:T(128)} %bitcast, s32[2048]{0:T(1024)S(1)} %fusion.21, s32[512]{0:T(512)} %param.7, bf16[512,1152]{1,0:T(8,128)(2,1)} %all-gather.3.cloned.1.call-done, bf16[2048,1152]{1,0:T(8,128)(2,1)} %all-gather.5.cloned.1.call-done), kind=kOutput, calls=%fused_computation.10 | convolution fusion | flops 2440036352 | bytes 10102804 | tf_op jit(solution)/shard_map/dot_general | solution.py:21
  130.2 0.0 copy-start.3
  130.2 2.1 copy-done.3
  132.3 0.0 copy-done
  132.3 0.0 copy-done.2
  132.3 0.0 copy-start.1
  132.3 5.5 %fusion.10 = f32[512,1152]{1,0:T(8,128)} fusion(bf16[2048,1152]{1,0:T(8,128)(2,1)S(1)} %copy-done, f32[512,2048]{1,0:T(8,128)S(1)} %get-tuple-element.6, f32[]{:T(128)} %bitcast.9, f32[]{:T(128)} %bitcast, s32[2048]{0:T(1024)S(1)} %fusion.21, s32[512]{0:T(512)S(1)} %copy-done.2), kind=kOutput, calls=%fused_computation.15 | convolution fusion | flops 2427453440 | bytes 11282440 | tf_op jit(solution)/shard_map/dot_general | solution.py:66
  137.7 0.0 reduce-scatter.3.cloned.1.call-update
  137.8 0.0 reduce-scatter.5.cloned.1.call-start
  137.8 0.0 copy-done.1
  137.8 9.7 %fusion.8 = f32[2048,1152]{1,0:T(8,128)} fusion(bf16[512,1152]{1,0:T(8,128)(2,1)S(1)} %copy-done.1, f32[512,2048]{1,0:T(8,128)} %copy-done.3, f32[]{:T(128)} %bitcast.11, f32[]{:T(128)} %bitcast, s32[2048]{0:T(1024)S(1)} %fusion.21, s32[512]{0:T(512)S(1)} %copy-done.2), kind=kOutput, calls=%fused_computation.13 | convolution fusion | flops 2427453440 | bytes 14821384 | tf_op jit(solution)/shard_map/dot_general | solution.py:67
  147.6 0.0 reduce-scatter.5.cloned.1.call-update
  147.6 1.9 pad_maximum_fusion
  149.5 84.3 %psum.7 = f32[3]{0:T(128)S(1)} all-reduce(f32[3]{0:T(128)S(1)} %pad_maximum_fusion), channel_id=1, replica_groups=mesh['grp'=32,'mem'=8] {'grp','mem'}, use_global_device_ids=true, to_apply=%region_5.6 | all-reduce | flops 3 | bytes 24 | tf_op jit(solution)/shard_map/psum | solution.py:74
  233.8 0.5 broadcast_multiply_fusion.2
  234.3 0.0 reduce-scatter.3.cloned.1.call-done
  234.3 1.7 broadcast_multiply_fusion.1
  236.0 74.2 %reduce-scatter.5.cloned.1.call-done = f32[64,1152]{1,0:T(8,128)} async-done(((f32[2048,1152]{1,0:T(8,128)}), f32[64,1152]{1,0:T(8,128)}) %reduce-scatter.5.cloned.1.call-update) | async-done | bytes 294928 | tf_op jit(solution)/shard_map/reduce_scatter | solution.py:72
  310.3 1.7 broadcast_multiply_fusion
  (1 shorter events, 0.0 us)
Async XLA Ops:
  7.2 43.5 %all-gather.3.cloned.1.call-start = ((), (), s32[]{:S(2)}) async-start(), calls=%async_computation.2 | async-start | bytes 1327104 | tf_op jit(solution)/shard_map/all_gather | solution.py:54
  7.9 112.2 %all-gather.5.cloned.1.call-start = ((), (), s32[]{:S(2)}) async-start(), calls=%async_computation.3 | async-start | bytes 4866048 | tf_op jit(solution)/shard_map/all_gather | solution.py:55
  8.6 225.7 %reduce-scatter.3.cloned.1.call-start = ((), (), s32[]{:S(2)}) async-start(), calls=%async_computation.4 | async-start | bytes 2654208 | tf_op jit(solution)/shard_map/reduce_scatter | solution.py:73
  120.1 12.2 %copy-start = (bf16[2048,1152]{1,0:T(8,128)(2,1)S(1)}, bf16[2048,1152]{1,0:T(8,128)(2,1)}, u32[]{:S(2)}) copy-start(bf16[2048,1152]{1,0:T(8,128)(2,1)} %all-gather.5.cloned.1.call-done) | copy-start | bytes 14155780
  120.1 12.2 %copy-start.2 = (s32[512]{0:T(512)S(1)}, s32[512]{0:T(512)}, u32[]{:S(2)}) copy-start(s32[512]{0:T(512)} %param.7) | copy-start | bytes 6148
  130.2 2.1 copy-start.3
  132.3 5.5 %copy-start.1 = (bf16[512,1152]{1,0:T(8,128)(2,1)S(1)}, bf16[512,1152]{1,0:T(8,128)(2,1)}, u32[]{:S(2)}) copy-start(bf16[512,1152]{1,0:T(8,128)(2,1)} %all-gather.3.cloned.1.call-done) | copy-start | bytes 3538948
  137.8 172.5 %reduce-scatter.5.cloned.1.call-start = ((), (), s32[]{:S(2)}) async-start(), calls=%async_computation.5 | async-start | bytes 9732096 | tf_op jit(solution)/shard_map/reduce_scatter | solution.py:72
Sparse Core Ops, SparseCore 0:
  9.8 40.8 all-gather.2
  53.2 66.8 all-gather.4
  137.9 38.6 reduce-scatter.2
  180.5 129.6 reduce-scatter.4
where the time goes:
time: 319 us
  waiting for transfers between devices  186 us (58%)
  blocking collectives  84.3 us (26%)
  matrix products  25.3 us (8%)
  between operations  15.1 us (5%)
  other arithmetic  5.83 us (2%)
    psum x1, blocking collectives, on_device(): totals = lax.psum(stat_sums, ('grp', 'mem'))  84.3 us
    reduce_scatter x1, waiting for transfers between devices, on_device(): lax.psum_scatter(text_acc, 'grp', scatter_dimension=0, tiled=True)  74.2 us
    all_gather x1, waiting for transfers between devices, on_device(): segment_part = lax.all_gather(caption_vectors, 'grp', axis=0, tiled=True)  69.4 us
    all_gather x1, waiting for transfers between devices, on_device(): images_in_group = lax.all_gather(picture_vectors, 'mem', axis=0, tiled=True)  40.6 us
    dot_general x1, matrix products, score_tile(): lax.dot_general(images_in_group, segment_part, (((1,), (1,)), ((), ())),...  10.1 us
    dot_general x1, matrix products, on_device(): lax.dot_general(coef_half, images_in_group, (((0,), (0,)), ((), ())), pre...  9.73 us
  transfers between devices with their start and end apart: 4, of which 3 were waited for; matrix products, arithmetic and copies ran while one was open for 4% of the time, Pallas kernels for 0%

commit v1 on v0

v1 whole, which is shorter than its diff:
```python
import jax
import jax.numpy as jnp
from jax import lax
from jax.experimental import pallas as pl
from jax.experimental.pallas import tpu as pltpu
from jax.sharding import PartitionSpec as P

MESH = pl.DeviceIdType.MESH
NX, NY, NZ = 4, 4, 8
ROWS = 64
HALF, QUARTER = 32, 16
D = 1152
TILE = 1024
PAIRS = 16384
LEVELS = 32000.0
BIAS = 256
BITS = 10

TEXT_ORDER = [(rx, ry) for rx in (2, 1, 3, 0) for ry in range(NY)]
IMAGE_ORDER = [
    (rc, rz) for part in ((4, 3, 5, 2), (6, 1, 7, 0)) for rc in (1, 0) for rz in part
]
TEXT_AT = {key: i * ROWS for i, key in enumerate(TEXT_ORDER)}
IMAGE_AT = {key: i * ROWS for i, key in enumerate(IMAGE_ORDER)}
N_COPIES = 256


def encode(values):
    top = jnp.max(jnp.abs(values), axis=1, keepdims=True)
    power = jnp.ceil(jnp.log2(jnp.maximum(top, 1e-36)))
    whole = jnp.round(values * (jnp.exp2(-power) * LEVELS)).astype(jnp.int32)
    lane = lax.broadcasted_iota(jnp.int32, (values.shape[0], 128), 1)
    code = power.astype(jnp.int32) + BIAS
    first = whole[:, :128]
    marked = (first & -2) | ((code >> jnp.minimum(lane, BITS)) & 1)
    first = jnp.where(lane < BITS, marked, first)
    return first.astype(jnp.int16), whole[:, 128:].astype(jnp.int16)


def decode(coded):
    whole = coded.astype(jnp.int32)
    lane = lax.broadcasted_iota(jnp.int32, (coded.shape[0], 128), 1)
    first = whole[:, :128]
    bits = jnp.where(lane < BITS, (first & 1) << jnp.minimum(lane, BITS), 0)
    code = jnp.sum(bits.astype(jnp.float32), axis=1, keepdims=True)
    return whole.astype(jnp.float32) * (jnp.exp2(code - BIAS) * (1.0 / LEVELS))


def fold(values):
    rows, columns = values.shape
    parts = [
        values[r : r + 8, c : c + 128]
        for r in range(0, rows, 8)
        for c in range(0, columns, 128)
    ]
    while len(parts) > 1:
        parts = [a + b for a, b in zip(parts[::2], parts[1::2], strict=True)]
    return parts[0]


def kernel(
    warmth_ref,
    offset_ref,
    labels_ref,
    image_hbm,
    text_hbm,
    image_out,
    text_out,
    stats_out,
    image,
    text,
    labels,
    label_row,
    scores,
    coef,
    image_sum,
    text_sum,
    coded_out,
    coded_in,
    stats,
    stat_slots,
    local_sem,
    send_sem,
    recv_sem,
):
    group, member = lax.axis_index("grp"), lax.axis_index("mem")
    core, x, z_high = lax.rem(group, 2), lax.rem(group // 2, NX), group // (2 * NX)
    y, z_low = lax.rem(member, NY), member // NY
    z = z_high * 2 + z_low

    def device(dx=0, dy=0, dz=0, dc=0):
        to_x, to_y = lax.rem(x + dx + NX, NX), lax.rem(y + dy + NY, NY)
        to_z, to_c = lax.rem(z + dz + NZ, NZ), lax.rem(core + dc, 2)
        return ((to_z // 2 * NX + to_x) * 2 + to_c, lax.rem(to_z, 2) * NY + to_y)

    right = {"x": device(dx=1), "y": device(dy=1), "z": device(dz=1)}
    left = {"x": device(dx=-1), "y": device(dy=-1), "z": device(dz=-1)}
    other = device(dc=1)

    image_at = {key: image.at[pl.ds(at, ROWS)] for key, at in IMAGE_AT.items()}
    own_image = pltpu.make_async_copy(image_hbm, image_at[0, 0], local_sem.at[0])
    own_text = pltpu.make_async_copy(
        text_hbm, text.at[pl.ds(TEXT_AT[0, 0], ROWS)], local_sem.at[1]
    )
    own_image.start()
    own_text.start()

    partners = [other]
    partners += [device(dx=d) for d in range(1, NX)]
    partners += [device(dy=d) for d in range(1, NY)]
    partners += [device(dz=d) for d in range(1, NZ)]
    barrier = pltpu.get_barrier_semaphore()
    for partner in partners:
        pl.semaphore_signal(barrier, inc=1, device_id=partner, device_id_type=MESH)
    pl.semaphore_wait(barrier, len(partners))

    copies = []

    def send(source, target, to):
        copy = pltpu.make_async_remote_copy(
            src_ref=source,
            dst_ref=target,
            send_sem=send_sem.at[len(copies)],
            recv_sem=recv_sem.at[len(copies)],
            device_id=to,
            device_id_type=MESH,
        )
        copies.append(copy)
        copy.start()
        return copy

    arrivals = {}

    def text_rows(key, row, rows):
        return text.at[pl.ds(TEXT_AT[key] + row, rows)]

    def send_text(key, row, rows, axis, step):
        rx, ry = key
        there = (
            ((rx - step) % NX, ry) if axis == "x" else (rx, (ry - step) % NY)
        )
        to = right[axis] if step == 1 else left[axis]
        arrivals[there, row] = send(
            text_rows(key, row, rows), text_rows(there, row, rows), to
        )

    def spread(key, row, rows, axis):
        send_text(key, row, rows, axis, 1)
        send_text(key, row, rows, axis, -1)

    def await_text(key, row):
        arrivals[key, row].wait_recv()

    def pass_on(key, row, axis):
        await_text(key, row)
        rel = key[0] if axis == "x" else key[1]
        if rel == 3:
            send_text(key, row, QUARTER, axis, 1)
        else:
            send_text(key, row + QUARTER, QUARTER, axis, -1)

    def send_image(key, row, rows, to, there):
        arrivals["image", there, row] = send(
            image.at[pl.ds(IMAGE_AT[key] + row, rows)],
            image.at[pl.ds(IMAGE_AT[there] + row, rows)],
            to,
        )

    own_text.wait()
    for row, axis in ((0, "x"), (HALF, "y")):
        spread((0, 0), row, HALF, axis)
    own_image.wait()
    send_image((0, 0), 0, ROWS, right["z"], (0, 7))
    send_image((0, 0), 0, ROWS, left["z"], (0, 1))
    for row, axis in ((0, "y"), (HALF, "x")):
        spread((0, 0), row, HALF, axis)
    send_image((0, 0), 0, ROWS, other, (1, 0))

    lane = lax.broadcasted_iota(jnp.int32, (8, 128), 1)
    mine = jnp.broadcast_to(labels_ref[pl.ds(member // 2, 1), :], (8, 128))
    turned = pltpu.roll(mine, 64, 1)
    in_upper = jnp.broadcast_to(lax.rem(member, 2), (8, 128)) == 1
    labels[0, 0] = jnp.where((lane >= 64) == in_upper, mine, turned)
    label_copies = []
    for d in range(1, NZ):
        label_copies.append(send(labels.at[0, 0], labels.at[0, NZ - d], device(dz=d)))

    def image_hop(rz):
        arrivals["image", (0, rz), 0].wait_recv()
        if rz in (7, 6):
            send_image((0, rz), 0, ROWS, right["z"], (0, rz - 1))
        elif rz == 5:
            send_image((0, rz), 0, HALF, right["z"], (0, 4))
        elif rz in (1, 2):
            send_image((0, rz), 0, ROWS, left["z"], (0, rz + 1))
        elif rz == 3:
            send_image((0, rz), HALF, HALF, left["z"], (0, 4))
        if rz == 4:
            arrivals["image", (0, 4), HALF].wait_recv()
        send_image((0, rz), 0, ROWS, other, (1, rz))

    for rel in (3, 1):
        pass_on((rel, 0), 0, "x")
        pass_on((0, rel), HALF, "y")
        spread((rel, 0), 0, HALF, "y")
        spread((0, rel), HALF, HALF, "x")
    image_hop(7)
    image_hop(1)
    for rel in (3, 1):
        pass_on((0, rel), 0, "y")
        pass_on((rel, 0), HALF, "x")
    for row in (0, QUARTER):
        await_text((2, 0), row)
        spread((2, 0), row, QUARTER, "y")
        await_text((0, 2), HALF + row)
        spread((0, 2), HALF + row, QUARTER, "x")
    image_hop(6)
    image_hop(2)
    for first in (3, 1):
        for rel in (3, 1):
            pass_on((first, rel), 0, "y")
            pass_on((rel, first), HALF, "x")
    image_hop(5)
    image_hop(3)
    for copy in label_copies:
        copy.wait_recv()
    label_other = send(labels.at[0], labels.at[1], other)
    for rel, row in ((3, 0), (1, QUARTER)):
        await_text((2, rel), row)
        send_text((2, rel), row, QUARTER, "y", 1 if rel == 3 else -1)
        await_text((rel, 2), HALF + row)
        send_text((rel, 2), HALF + row, QUARTER, "x", 1 if rel == 3 else -1)
    image_hop(4)
    await_text((2, 3), QUARTER)
    await_text((2, 1), 0)
    await_text((3, 2), HALF + QUARTER)
    await_text((1, 2), HALF)
    for rel in range(NX):
        await_text((rel, 2), 0)
        await_text((rel, 2), QUARTER)
        await_text((2, rel), HALF)
        await_text((2, rel), HALF + QUARTER)
    for rz in range(NZ):
        arrivals["image", (1, rz), 0].wait_recv()
    label_other.wait_recv()

    for at in range(0, TILE // ROWS, 2):
        (ca, za), (cb, zb) = IMAGE_ORDER[at], IMAGE_ORDER[at + 1]
        label_row[:, at * ROWS : (at + 2) * ROWS] = jnp.where(
            lane < 64, labels[ca, za], labels[cb, zb]
        )

    warmth = jnp.exp(jnp.full((1, 1), warmth_ref[0], jnp.float32))
    offset = offset_ref[0]
    zero = jnp.zeros((8, 128), jnp.float32)
    for i in range(3):
        stats[i] = zero

    def pairs(chunk):
        first = chunk * 256
        slot = chunk % 2
        scores[slot] = lax.dot_general(
            text[pl.ds(first, 256), :],
            image[...],
            (((1,), (1,)), ((), ())),
            preferred_element_type=jnp.float32,
        )
        for row in range(0, 256, 32):
            rx, ry = TEXT_ORDER[(first + row) // ROWS]
            owner_x, owner_y = lax.rem(x + rx, NX), lax.rem(y + ry, NY)
            base = (
                ((z_high * NX + owner_x) * 2 + core) * 8 + z_low * NY + owner_y
            ) * ROWS + row % ROWS
            position = lax.broadcasted_iota(jnp.int32, (32, 1), 0) + base
            for column in range(0, TILE, 256):
                at = pl.ds(column, 256)
                s = scores[slot, pl.ds(row, 32), at]
                logit = s * warmth + offset
                matched = label_row[0:1, at] == position
                signed = jnp.where(matched, -logit, logit)
                e = jnp.exp(-jnp.abs(signed))
                one_e = 1.0 + e
                inverse = 1.0 / one_e
                chance = jnp.where(signed >= 0, inverse, e * inverse)
                factor = jnp.where(matched, -chance, chance)
                coef[pl.ds(first + row, 32), at] = factor.astype(jnp.bfloat16)
                grown = zero
                for r in range(0, 32, 8):
                    for c in range(0, 256, 128):
                        part = slice(r, r + 8), slice(c, c + 128)
                        grown = grown * one_e[part] + e[part]
                stats[0] += fold(jnp.maximum(signed, 0.0)) + jnp.log1p(grown)
                stats[1] += fold(factor * s)
                stats[2] += fold(factor)

    def text_part(chunk):
        at = pl.ds(chunk * 256, 256)
        text_sum[at, :] = jnp.dot(
            coef[at, :], image[...], preferred_element_type=jnp.float32
        )

    def image_part(chunk):
        at = pl.ds(chunk * 256, 256)
        image_sum[at, :] = lax.dot_general(
            coef[:, at],
            text[...],
            (((0,), (0,)), ((), ())),
            preferred_element_type=jnp.float32,
        )

    place = [0]

    def send_sum(source, at, rows, to):
        start = place[0]
        place[0] += rows
        for r in range(0, rows, QUARTER):
            low, high = encode(source[pl.ds(at + r, QUARTER), :])
            coded_out[pl.ds(start + r, QUARTER), :128] = low
            coded_out[pl.ds(start + r, QUARTER), 128:] = high
        copy = send(
            coded_out.at[pl.ds(start, rows)], coded_in.at[pl.ds(start, rows)], to
        )
        return copy, start, rows

    def add_sum(sent, target, at):
        copy, start, rows = sent
        copy.wait_recv()
        for r in range(0, rows, QUARTER):
            target[pl.ds(at + r, QUARTER), :] += decode(
                coded_in[pl.ds(start + r, QUARTER), :]
            )

    def text_ring(axis, row, line):
        far, ahead, behind, here = (TEXT_AT[line[i]] + row for i in (2, 1, 3, 0))
        sent = {}

        def one():
            sent[1] = send_sum(text_sum, far, QUARTER, right[axis])
            sent[2] = send_sum(text_sum, far + QUARTER, QUARTER, left[axis])

        def two():
            add_sum(sent[1], text_sum, ahead)
            sent[3] = send_sum(text_sum, ahead, HALF, right[axis])
            add_sum(sent[2], text_sum, behind + QUARTER)
            sent[4] = send_sum(text_sum, behind, HALF, left[axis])

        def three():
            add_sum(sent[3], text_sum, here)
            add_sum(sent[4], text_sum, here)

        return one, two, three

    along_y = {rx: text_ring("y", 0, [(rx, i) for i in range(NY)]) for rx in range(NX)}
    along_x = {
        ry: text_ring("x", HALF, [(i, ry) for i in range(NX)]) for ry in range(NY)
    }
    last_x = text_ring("x", 0, [(i, 0) for i in range(NX)])
    last_y = text_ring("y", HALF, [(0, i) for i in range(NY)])

    for chunk in range(4):
        pairs(chunk)
    text_part(0)
    along_y[2][0]()
    for ry in (2, 1, 3, 0):
        along_x[ry][0]()
    text_part(1)
    along_y[1][0]()
    along_y[2][1]()
    text_part(2)
    along_y[3][0]()
    for ry in (2, 1, 3, 0):
        along_x[ry][1]()
    text_part(3)
    along_y[0][0]()
    along_y[1][1]()
    along_y[3][1]()
    along_y[2][2]()
    along_y[0][1]()

    sent_other = {}
    sent_z = {}

    def to_other(part):
        for rz in part:
            sent_other[rz] = send_sum(image_sum, IMAGE_AT[1, rz], ROWS, other)

    def from_other(part):
        for rz in part:
            add_sum(sent_other[rz], image_sum, IMAGE_AT[0, rz])

    def z_send(rz, row, to):
        sent_z[rz, row] = send_sum(image_sum, IMAGE_AT[0, rz] + row, HALF, to)

    def z_add(rz, row, target):
        add_sum(sent_z[rz, row], image_sum, IMAGE_AT[0, target] + row)

    image_part(0)
    to_other((4, 3, 5, 2))
    image_part(1)
    from_other((4, 3, 5, 2))
    z_send(4, 0, right["z"])
    z_send(4, HALF, left["z"])
    z_send(3, HALF, right["z"])
    z_send(5, 0, left["z"])
    image_part(2)
    to_other((6, 1, 7, 0))
    z_add(4, 0, 3)
    z_send(3, 0, right["z"])
    z_add(4, HALF, 5)
    z_send(5, HALF, left["z"])
    along_x[2][2]()
    last_y[0]()
    along_y[1][2]()
    along_y[3][2]()
    last_x[0]()
    image_part(3)
    from_other((6, 1, 7, 0))
    z_add(3, HALF, 2)
    z_send(2, HALF, right["z"])
    z_add(5, 0, 6)
    z_send(6, 0, left["z"])
    z_add(3, 0, 2)
    z_send(2, 0, right["z"])
    z_add(5, HALF, 6)
    z_send(6, HALF, left["z"])
    along_x[1][2]()
    along_x[3][2]()
    last_y[1]()
    last_x[1]()
    z_add(2, HALF, 1)
    z_send(1, HALF, right["z"])
    z_add(6, 0, 7)
    z_send(7, 0, left["z"])
    z_add(2, 0, 1)
    z_send(1, 0, right["z"])
    z_add(6, HALF, 7)
    z_send(7, HALF, left["z"])

    def total(slot):
        return jnp.concatenate(
            [jnp.sum(stats[i], axis=0, keepdims=True) for i in range(3)]
            + [jnp.zeros((5, 128), jnp.float32)],
            axis=0,
        ) if slot is None else slot

    running = total(None)
    base = 0
    for size, me, to in (
        (2, core, lambda d: device(dc=d)),
        (NX, x, lambda d: device(dx=d)),
        (NY, y, lambda d: device(dy=d)),
        (NZ, z, lambda d: device(dz=d)),
    ):
        stat_slots[base + me] = running
        sent = [
            send(stat_slots.at[base + me], stat_slots.at[base + me], to(d))
            for d in range(1, size)
        ]
        for copy in sent:
            copy.wait_recv()
        running = stat_slots[base]
        for i in range(1, size):
            running = running + stat_slots[base + i]
        base += size
    share = 1.0 / float(PAIRS * PAIRS)
    stats_out[0] = jnp.sum(running[0:1, :]) * share
    stats_out[1] = jnp.sum(running[1:2, :] * warmth) * share
    stats_out[2] = jnp.sum(running[2:3, :]) * share

    along_x[0][2]()
    along_y[0][2]()
    last_x[2]()
    last_y[2]()
    stretch = warmth * (1.0 / PAIRS)
    text_out[...] = text_sum[pl.ds(TEXT_AT[0, 0], ROWS), :] * stretch
    for row in (HALF, 0):
        z_add(1, row, 0)
    for row in (0, HALF):
        z_add(7, row, 0)
    image_out[...] = image_sum[pl.ds(IMAGE_AT[0, 0], ROWS), :] * stretch
    for copy in copies:
        copy.wait_send()


def on_device(picture, caption, labels, warmth, offset):
    vmem = pl.BlockSpec(memory_space=pltpu.VMEM)
    smem = pl.BlockSpec(memory_space=pltpu.SMEM)
    hbm = pl.BlockSpec(memory_space=pl.ANY)
    grad = jax.ShapeDtypeStruct((ROWS, D), jnp.float32)
    return pl.pallas_call(
        kernel,
        out_shape=(grad, grad, jax.ShapeDtypeStruct((3,), jnp.float32)),
        in_specs=[smem, smem, vmem, hbm, hbm],
        out_specs=(vmem, vmem, smem),
        scratch_shapes=[
            pltpu.VMEM((TILE, D), jnp.bfloat16),
            pltpu.VMEM((TILE, D), jnp.bfloat16),
            pltpu.VMEM((2, NZ, 8, 128), jnp.int32),
            pltpu.VMEM((8, TILE), jnp.int32),
            pltpu.VMEM((2, 256, TILE), jnp.float32),
            pltpu.VMEM((TILE, TILE), jnp.bfloat16),
            pltpu.VMEM((TILE, D), jnp.float32),
            pltpu.VMEM((TILE, D), jnp.float32),
            pltpu.VMEM((2048, D), jnp.int16),
            pltpu.VMEM((2048, D), jnp.int16),
            pltpu.VMEM((3, 8, 128), jnp.float32),
            pltpu.VMEM((2 + NX + NY + NZ, 8, 128), jnp.float32),
            pltpu.SemaphoreType.DMA((2,)),
            pltpu.SemaphoreType.DMA((N_COPIES,)),
            pltpu.SemaphoreType.DMA((N_COPIES,)),
        ],
        compiler_params=pltpu.CompilerParams(
            collective_id=0, has_side_effects=True, vmem_limit_bytes=56 << 20
        ),
    )(warmth, offset, labels.reshape(4, 128), picture, caption)


def solution(mesh):
    rows = P(("grp", "mem"), None)
    return jax.shard_map(
        on_device,
        mesh=mesh,
        in_specs=(rows, rows, P("grp"), P(), P()),
        out_specs=(rows, rows, P()),
        check_vma=False,
    )
```

time: 319 us -> 86.9 us (0.27)
  waiting for transfers between devices: 186 us -> 0 us
  blocking collectives: 84.3 us -> 0 us
  Pallas kernels: 0 us -> 81.8 us
  matrix products: 25.3 us -> 0 us
  between operations: 15.1 us -> 1.94 us
  other arithmetic: 5.83 us -> 0 us
    all_gather x2 -> x0, waiting for transfers between devices: 110 us -> none  [the longest x1 69.4 us: on_device(): segment_part = lax.all_gather(caption_vectors, 'grp', axis=0, tiled=True)]
    psum x1 -> x0, blocking collectives: 84.3 us -> none  [on_device(): totals = lax.psum(stat_sums, ('grp', 'mem'))]
    pallas_call x0 -> x1, Pallas kernels: none -> 81.8 us  [on_device(): pl.pallas_call(kernel, out_shape=(grad, grad, jax.ShapeDtypeStruct((3,),...]
    reduce_scatter x2 -> x0, waiting for transfers between devices: 74.2 us -> none  [the longest x1 74.2 us: on_device(): lax.psum_scatter(text_acc, 'grp', scatter_dimension=0, tiled=True)]
    dot_general x3 -> x0, matrix products: 25.3 us -> none  [the longest x1 10.1 us: score_tile(): lax.dot_general(images_in_group, segment_part, (((1,), (1,)), ((), ())),...]
    mul x2 -> x0, other arithmetic: 3.39 us -> none  [the longest x1 1.7 us: on_device(): image_grad = image_total * stretch_factor]
  transfers between devices with their start and end apart: 4 -> 0, of which waited for: 3 -> 0; matrix products, arithmetic and copies ran while one was open for 4% -> 0% of each run, Pallas kernels for 0% -> 0%
where the time goes in v1:
time: 86.9 us; the launch traced here: 86.7 us
  Pallas kernels  81.8 us (94%)
  local copies, waits for them, and re-layouts  2.97 us (3%)
  between operations  1.94 us (2%)
    pallas_call x1, Pallas kernels, on_device(): pl.pallas_call(kernel, out_shape=(grad, grad, jax.ShapeDtypeStruct((3,),...  81.8 us
    unnamed x7, local copies, waits for them, and re-layouts  2.97 us

profile of v1, /device:TPU:1, one launch (start us, length us, event | category | flops | bytes accessed | tf_op | source)
XLA Modules:
  0.0 86.7 jit_solution(15408212382850035174)
XLA Ops:
  1.9 81.8 %shard_map.76 = (f32[64,1152]{1,0:T(8,128)}, f32[64,1152]{1,0:T(8,128)}, f32[3]{0:T(128)}) custom-call(f32[1]{0:T(128)S(6)} %copy.11.warmth_ref, f32[1]{0:T(128)S(6)} %copy.12.offset_ref, s32[4,128]{1,0:T(4,128)} %bitcast.1, bf16[64,1152]{1,0:T(8,128)(2,1)} %image_hbm.1, bf16[64,1152]{1,0:T(8,128)(2,1)} %text_hbm.1), custom_call_target="tpu_custom_call" | custom-call | tf_op jit(solution)/shard_map/pallas_call | solution.py:490
  83.7 0.0 copy-start
  83.7 1.7 %copy.13 = f32[64,1152]{1,0:T(8,128)} copy(f32[64,1152]{1,0:T(8,128)} %get-tuple-element.6) | data formatting | bytes 589824
  85.5 0.0 copy-done
  85.5 0.0 copy-start.1
  85.5 0.7 copy.14
  86.2 0.0 copy-done.1
  86.2 0.5 copy.15
Async XLA Ops:
  83.7 1.8 %copy-start = (f32[64,1152]{1,0:T(8,128)S(1)}, f32[64,1152]{1,0:T(8,128)}, u32[]{:S(2)}) copy-start(f32[64,1152]{1,0:T(8,128)} %get-tuple-element.7) | copy-start | bytes 884740
  85.5 0.7 copy-start.1

commit v2 on v0

v2 whole, which is shorter than its diff:
```python
import jax
import jax.numpy as jnp
from jax import lax
from jax.experimental import pallas as pl
from jax.experimental.pallas import tpu as pltpu
from jax.sharding import PartitionSpec as P

MESH = pl.DeviceIdType.MESH
NX, NY, NZ = 4, 4, 8
ROWS = 64
HALF, QUARTER = 32, 16
D = 1152
LANES = 128
WIDE = D // LANES
TILE = 1024
PAIRS = 16384
LEVELS = 32000.0
SMALLEST = 1e-30

FAR_FIRST = (2, 1, 3, 0)
TEXT_HALVES = [
    (h, i, j)
    for i in FAR_FIRST
    for h in (0, 1)
    for j in (FAR_FIRST if h == 0 else FAR_FIRST[::-1])
]
TEXT_AT = {key: n * HALF for n, key in enumerate(TEXT_HALVES)}
IMAGE_ORDER = [
    (c, d) for part in ((4, 3, 5, 2), (6, 1, 7, 0)) for c in (1, 0) for d in part
]
IMAGE_AT = {key: n * ROWS for n, key in enumerate(IMAGE_ORDER)}
N_SEND, N_RECV = 6, 91
N_TILES = 1142


def fold(values):
    rows, columns = values.shape
    parts = [
        values[r : r + 8, c : c + LANES]
        for r in range(0, rows, 8)
        for c in range(0, columns, LANES)
    ]
    while len(parts) > 1:
        parts = [a + b for a, b in zip(parts[::2], parts[1::2], strict=True)]
    return parts[0]


def kernel(
    warmth_ref,
    offset_ref,
    labels_ref,
    image_hbm,
    text_hbm,
    image_out,
    text_out,
    stats_out,
    image,
    text,
    labels,
    label_row,
    scores,
    coef,
    image_sum,
    text_sum,
    image_top,
    text_top,
    coded_out,
    coded_in,
    stats,
    stat_slots,
    local_sem,
    send_sem,
    recv_sem,
):
    group, member = lax.axis_index("grp"), lax.axis_index("mem")
    core, x, z_high = lax.rem(group, 2), lax.rem(group // 2, NX), group // (2 * NX)
    y, z_low = lax.rem(member, NY), member // NY
    z = z_high * 2 + z_low

    def device(dx=0, dy=0, dz=0, dc=0):
        to_x, to_y = lax.rem(x + dx + NX, NX), lax.rem(y + dy + NY, NY)
        to_z, to_c = lax.rem(z + dz + NZ, NZ), lax.rem(core + dc, 2)
        return ((to_z // 2 * NX + to_x) * 2 + to_c, lax.rem(to_z, 2) * NY + to_y)

    ahead = {"x": device(dx=1), "y": device(dy=1), "z": device(dz=1)}
    behind = {"x": device(dx=-1), "y": device(dy=-1), "z": device(dz=-1)}
    other = device(dc=1)

    own_image = pltpu.make_async_copy(
        image_hbm, image.at[pl.ds(IMAGE_AT[0, 0], ROWS)], local_sem.at[0]
    )
    own_text = pltpu.make_async_copy(
        text_hbm, text.at[pl.ds(TEXT_AT[0, 0, 0], ROWS)], local_sem.at[1]
    )
    own_image.start()
    own_text.start()

    partners = [other]
    partners += [device(dx=d) for d in range(1, NX)]
    partners += [device(dy=d) for d in range(1, NY)]
    partners += [device(dz=d) for d in range(1, NZ)]
    barrier = pltpu.get_barrier_semaphore()
    for partner in partners:
        pl.semaphore_signal(barrier, inc=1, device_id=partner, device_id_type=MESH)
    pl.semaphore_wait(barrier, len(partners))

    recv_of, sent_of = {}, {}

    def place(key):
        return recv_sem.at[recv_of.setdefault(key, len(recv_of))]

    def send(kind, amount, source, target, to, key):
        at = list(sent_of).index(kind) if kind in sent_of else len(sent_of)
        sent_of[kind] = sent_of.get(kind, 0) + amount
        pltpu.make_async_remote_copy(
            src_ref=source,
            dst_ref=target,
            send_sem=send_sem.at[at],
            recv_sem=place(key),
            device_id=to,
            device_id_type=MESH,
        ).start()

    def expect(key, ref):
        pltpu.make_async_remote_copy(
            src_ref=ref,
            dst_ref=ref,
            send_sem=send_sem.at[0],
            recv_sem=place(key),
            device_id=other,
            device_id_type=MESH,
        ).wait_recv()

    def all_sent(refs):
        for at, (kind, amount) in enumerate(sent_of.items()):
            ref = refs[kind].at[pl.ds(0, amount)]
            pltpu.make_async_remote_copy(
                src_ref=ref,
                dst_ref=ref,
                send_sem=send_sem.at[at],
                recv_sem=recv_sem.at[0],
                device_id=other,
                device_id_type=MESH,
            ).wait_send()

    def axis_of(h, nth):
        return "xy"[(h + nth) % 2]

    def text_key(h, i, j):
        return ("rest", h) if j == 2 else ("text", h, i, j)

    def send_text(h, i, j, row, rows, nth, step):
        there = (h, (i - step) % 4, j) if nth == 0 else (h, i, (j - step) % 4)
        send(
            "text",
            rows,
            text.at[pl.ds(TEXT_AT[h, i, j] + row, rows)],
            text.at[pl.ds(TEXT_AT[there] + row, rows)],
            (ahead if step == 1 else behind)[axis_of(h, nth)],
            text_key(*there),
        )

    def spread(h, i, j, nth):
        send_text(h, i, j, 0, HALF, nth, 1)
        send_text(h, i, j, 0, HALF, nth, -1)

    def await_text(h, i, j):
        expect(text_key(h, i, j), text.at[pl.ds(0, HALF)])

    def pass_on(h, i, j, nth):
        if (i, j)[nth] == 3:
            send_text(h, i, j, 0, QUARTER, nth, 1)
        else:
            send_text(h, i, j, QUARTER, QUARTER, nth, -1)

    def send_image(c, d, row, to, there):
        send(
            "image",
            HALF,
            image.at[pl.ds(IMAGE_AT[c, d] + row, HALF)],
            image.at[pl.ds(IMAGE_AT[there] + row, HALF)],
            to,
            "across" if there[0] else ("image", there[1], row),
        )

    def image_hop(d, row):
        expect(("image", d, row), image.at[pl.ds(0, HALF)])
        if d > 5 or (d == 5 and row == 0):
            send_image(0, d, row, ahead["z"], (0, d - 1))
        if d < 3 or (d == 3 and row == HALF):
            send_image(0, d, row, behind["z"], (0, d + 1))
        send_image(0, d, row, other, (1, d))

    own_text.wait()
    for h in (0, 1):
        spread(h, 0, 0, 0)
    own_image.wait()
    send_image(0, 0, 0, ahead["z"], (0, 7))
    send_image(0, 0, HALF, behind["z"], (0, 1))
    for h in (0, 1):
        spread(h, 0, 0, 1)
    send_image(0, 0, HALF, ahead["z"], (0, 7))
    send_image(0, 0, 0, behind["z"], (0, 1))
    for row in (0, HALF):
        send_image(0, 0, row, other, (1, 0))

    lane = lax.broadcasted_iota(jnp.int32, (8, LANES), 1)
    mine = jnp.broadcast_to(labels_ref[pl.ds(member // 2, 1), :], (8, LANES))
    turned = pltpu.roll(mine, ROWS, 1)
    in_upper = jnp.broadcast_to(lax.rem(member, 2), (8, LANES)) == 1
    labels[0, 0] = jnp.where((lane >= ROWS) == in_upper, mine, turned)
    for d in range(1, NZ):
        there = labels.at[0, NZ - d]
        send("label", 1, labels.at[0, 0], there, device(dz=d), "label")

    for i in (3, 1):
        for h in (0, 1):
            await_text(h, i, 0)
            pass_on(h, i, 0, 0)
            spread(h, i, 0, 1)
    image_hop(7, 0)
    image_hop(1, HALF)
    for j in (3, 1):
        for h in (0, 1):
            await_text(h, 0, j)
            pass_on(h, 0, j, 1)
    image_hop(7, HALF)
    image_hop(1, 0)
    for h in (0, 1):
        await_text(h, 2, 0)
        spread(h, 2, 0, 1)
    image_hop(6, 0)
    image_hop(2, HALF)
    for i in (3, 1):
        for j in (3, 1):
            for h in (0, 1):
                await_text(h, i, j)
                pass_on(h, i, j, 1)
        image_hop((6, 5)[i == 1], (HALF, 0)[i == 1])
        image_hop((2, 3)[i == 1], (0, HALF)[i == 1])
    expect("label", labels.at[0, pl.ds(1, NZ - 1)])
    send("labels", 1, labels.at[pl.ds(0, 1)], labels.at[pl.ds(1, 1)], other, "labels")
    image_hop(5, HALF)
    image_hop(3, 0)
    for j in (3, 1):
        for h in (0, 1):
            await_text(h, 2, j)
            pass_on(h, 2, j, 1)
    image_hop(4, 0)
    image_hop(4, HALF)
    for h in (0, 1):
        expect(("rest", h), text.at[pl.ds(0, 4 * HALF)])
    expect("labels", labels.at[pl.ds(0, 1)])
    expect("across", image.at[pl.ds(0, NZ * ROWS)])

    for at in range(0, TILE // ROWS, 2):
        label_row[:, at * ROWS : (at + 2) * ROWS] = jnp.where(
            lane < ROWS, labels[IMAGE_ORDER[at]], labels[IMAGE_ORDER[at + 1]]
        )

    warmth = jnp.exp(jnp.full((1, 1), warmth_ref[0], jnp.float32))
    offset = offset_ref[0]
    zero = jnp.zeros((8, LANES), jnp.float32)
    for n in range(3):
        stats[n] = zero

    def pairs(chunk):
        first = chunk * 256
        slot = chunk % 2
        scores[slot] = lax.dot_general(
            text[pl.ds(first, 256), :],
            image[...],
            (((1,), (1,)), ((), ())),
            preferred_element_type=jnp.float32,
        )
        for row in range(0, 256, HALF):
            h, i, j = TEXT_HALVES[(first + row) // HALF]
            rx, ry = (i, j) if h == 0 else (j, i)
            owner_x, owner_y = lax.rem(x + rx, NX), lax.rem(y + ry, NY)
            base = (
                ((z_high * NX + owner_x) * 2 + core) * 8 + z_low * NY + owner_y
            ) * ROWS + h * HALF
            position = lax.broadcasted_iota(jnp.int32, (HALF, 1), 0) + base
            for column in range(0, TILE, 256):
                at = pl.ds(column, 256)
                s = scores[slot, pl.ds(row, HALF), at]
                logit = s * warmth + offset
                matched = label_row[0:1, at] == position
                signed = jnp.where(matched, -logit, logit)
                e = jnp.exp(-jnp.abs(signed))
                one_e = 1.0 + e
                inverse = 1.0 / one_e
                chance = jnp.where(signed >= 0, inverse, e * inverse)
                factor = jnp.where(matched, -chance, chance)
                coef[pl.ds(first + row, HALF), at] = factor.astype(jnp.bfloat16)
                grown = zero
                for r in range(0, HALF, 8):
                    for c in range(0, 256, LANES):
                        part = slice(r, r + 8), slice(c, c + LANES)
                        grown = grown * one_e[part] + e[part]
                stats[0] += fold(jnp.maximum(signed, 0.0)) + jnp.log1p(grown)
                stats[1] += fold(factor * s)
                stats[2] += fold(factor)

    def find_tops(sums, tops, first):
        for row in range(first, first + 256, HALF):
            top = None
            for r in range(0, HALF, 8):
                for c in range(0, D, LANES):
                    part = jnp.abs(sums[pl.ds(row + r, 8), c : c + LANES])
                    top = part if top is None else jnp.maximum(top, part)
            top = jnp.max(jnp.max(top, axis=1, keepdims=True), axis=0, keepdims=True)
            tops[row // HALF] = jnp.broadcast_to(top, (QUARTER, LANES))

    def text_part(chunk):
        at = pl.ds(chunk * 256, 256)
        text_sum[at, :] = jnp.dot(
            coef[at, :], image[...], preferred_element_type=jnp.float32
        )
        find_tops(text_sum, text_top, chunk * 256)

    def image_part(chunk):
        at = pl.ds(chunk * 256, 256)
        image_sum[at, :] = lax.dot_general(
            coef[:, at],
            text[...],
            (((0,), (0,)), ((), ())),
            preferred_element_type=jnp.float32,
        )
        find_tops(image_sum, image_top, chunk * 256)

    messages = {}
    used = [0]

    def arrived(parts):
        found = {}
        for adds in parts:
            for name, _ in adds:
                power = coded_in[messages[name]].astype(jnp.float32)
                bound = jnp.exp2(power)
                found[name] = bound * (1.0 / LEVELS), bound
        return found

    def summed(sums, row, wide, adds, found):
        value = sums[pl.ds(row, QUARTER), wide * LANES : (wide + 1) * LANES]
        for name, nth in adds:
            tile = coded_in[messages[name] + 1 + nth * WIDE + wide]
            value = value + tile.astype(jnp.float32) * found[name][0]
        return value

    def send_sum(name, sums, tops, row, parts, to, key):
        start, count = used[0], 1 + len(parts) * WIDE
        messages[name] = start
        used[0] += count
        found = arrived(parts)
        bound = tops[row // HALF]
        if len(parts) * QUARTER > HALF:
            bound = jnp.maximum(bound, tops[row // HALF + 1])
        for _, more in found.values():
            bound = bound + more
        power = jnp.ceil(jnp.log2(jnp.maximum(bound, SMALLEST)))
        coded_out[start] = power.astype(jnp.int16)
        scale = jnp.exp2(-power) * LEVELS
        for n, adds in enumerate(parts):
            for wide in range(WIDE):
                value = summed(sums, row + n * QUARTER, wide, adds, found)
                coded_out[start + 1 + n * WIDE + wide] = (
                    jnp.round(value * scale).astype(jnp.int32).astype(jnp.int16)
                )
        at = pl.ds(start, count)
        send("sum", count, coded_out.at[at], coded_in.at[at], to, key)

    def await_sum(key, *sizes):
        count = sum(1 + rows // QUARTER * WIDE for rows in sizes)
        expect(key, coded_in.at[pl.ds(0, count)])

    def text_send(name, at, row, parts, to):
        send_sum(name, text_sum, text_top, at + row, parts, to, name)

    def second_far(i):
        for h in (0, 1):
            axis, at = axis_of(h, 1), TEXT_AT[h, i, 2]
            text_send((h, i, "fa"), at, 0, [[]], ahead[axis])
            text_send((h, i, "fb"), at, QUARTER, [[]], behind[axis])

    def second_near(i):
        for h in (0, 1):
            axis = axis_of(h, 1)
            await_sum((h, i, "fa"), QUARTER)
            parts = [[((h, i, "fa"), 0)], []]
            name = (h, i, "na")
            send_sum(
                name, text_sum, text_top, TEXT_AT[h, i, 1], parts, ahead[axis], (h, i, "n")
            )
            await_sum((h, i, "fb"), QUARTER)
            parts = [[], [((h, i, "fb"), 0)]]
            name = (h, i, "nb")
            send_sum(
                name, text_sum, text_top, TEXT_AT[h, i, 3], parts, behind[axis], (h, i, "n")
            )

    def second_done(i):
        for h in (0, 1):
            await_sum((h, i, "n"), HALF, HALF)

    def line(h, i, nth):
        return [((h, i, "na"), nth), ((h, i, "nb"), nth)]

    def first_far():
        for h in (0, 1):
            axis, at = axis_of(h, 0), TEXT_AT[h, 2, 0]
            text_send((h, "fa"), at, 0, [line(h, 2, 0)], ahead[axis])
            text_send((h, "fb"), at, QUARTER, [line(h, 2, 1)], behind[axis])

    def first_near(i):
        for h in (0, 1):
            axis = axis_of(h, 0)
            far = "fa" if i == 1 else "fb"
            await_sum((h, far), QUARTER)
            parts = [line(h, i, 0), line(h, i, 1)]
            parts[i == 3].append(((h, far), 0))
            send_sum(
                (h, "n", i),
                text_sum,
                text_top,
                TEXT_AT[h, i, 0],
                parts,
                (ahead if i == 1 else behind)[axis],
                (h, "n"),
            )

    def text_last():
        for h in (0, 1):
            await_sum((h, "n"), HALF, HALF)
            for n in (0, 1):
                adds = line(h, 0, n) + [((h, "n", 1), n), ((h, "n", 3), n)]
                found = arrived([adds])
                at = h * HALF + n * QUARTER
                for wide in range(WIDE):
                    value = summed(
                        text_sum, TEXT_AT[h, 0, 0] + n * QUARTER, wide, adds, found
                    )
                    text_out[at : at + QUARTER, wide * LANES : (wide + 1) * LANES] = (
                        value * stretch
                    )

    def to_other(part):
        for d in part:
            send_sum(
                ("c", d), image_sum, image_top, IMAGE_AT[1, d], [[]] * 4, other, ("c", part)
            )

    def from_other(part):
        await_sum(("c", part), *[ROWS] * len(part))

    def z_adds(d, row, n):
        adds = [(("c", d), row // QUARTER + n)]
        if d < 4 and (d < 3 or row == 0):
            adds.append((("za", d + 1, row), n))
        if (d > 4 or d == 0) and (d != 5 or row == HALF):
            adds.append((("zb", (d - 1) % NZ, row), n))
        return adds

    def z_send(d, row, way, wait=True):
        came = [a[0] for a in z_adds(d, row, 0)[1:]]
        for name in came:
            await_sum(name, HALF)
        name = ("z" + way, d, row)
        parts = [z_adds(d, row, n) for n in (0, 1)]
        to = (ahead if way == "a" else behind)["z"]
        send_sum(name, image_sum, image_top, IMAGE_AT[0, d] + row, parts, to, name)

    def image_last():
        for row in (0, HALF):
            for name in (("za", 1, row), ("zb", 7, row)):
                await_sum(name, HALF)
            for n in (0, 1):
                adds = z_adds(0, row, n)
                found = arrived([adds])
                at = row + n * QUARTER
                for wide in range(WIDE):
                    value = summed(
                        image_sum, IMAGE_AT[0, 0] + at, wide, adds, found
                    )
                    image_out[at : at + QUARTER, wide * LANES : (wide + 1) * LANES] = (
                        value * stretch
                    )

    stat_axes = (
        (2, core, lambda d: device(dc=d)),
        (NX, x, lambda d: device(dx=d)),
        (NY, y, lambda d: device(dy=d)),
        (NZ, z, lambda d: device(dz=d)),
    )

    def stat_send(nth, value):
        base = sum(a[0] for a in stat_axes[:nth])
        size, me, to = stat_axes[nth]
        stat_slots[base + me] = value
        for d in range(1, size):
            slot = stat_slots.at[pl.ds(base + me, 1)]
            send("stat", 1, slot, slot, to(d), ("stat", nth))

    def stat_sum(nth):
        base, size = sum(a[0] for a in stat_axes[:nth]), stat_axes[nth][0]
        expect(("stat", nth), stat_slots.at[pl.ds(0, size - 1)])
        value = stat_slots[base]
        for n in range(1, size):
            value = value + stat_slots[base + n]
        return value

    stretch = warmth * (1.0 / PAIRS)
    near_part, far_part = (6, 1, 7, 0), (4, 3, 5, 2)

    for chunk in range(4):
        pairs(chunk)
    stat_send(
        0,
        jnp.concatenate(
            [jnp.sum(stats[n], axis=0, keepdims=True) for n in range(3)]
            + [jnp.zeros((5, LANES), jnp.float32)],
            axis=0,
        ),
    )
    image_part(0)
    to_other(far_part)
    text_part(0)
    second_far(2)
    image_part(1)
    stat_send(1, stat_sum(0))
    from_other(far_part)
    z_send(4, 0, "a")
    z_send(4, HALF, "b")
    z_send(3, HALF, "a")
    z_send(5, 0, "b")
    text_part(1)
    second_far(1)
    second_near(2)
    image_part(2)
    to_other(near_part)
    stat_send(2, stat_sum(1))
    z_send(3, 0, "a")
    z_send(5, HALF, "b")
    text_part(2)
    second_far(3)
    second_near(1)
    second_done(2)
    first_far()
    z_send(2, HALF, "a")
    text_part(3)
    second_far(0)
    second_near(3)
    image_part(3)
    from_other(near_part)
    z_send(6, 0, "b")
    z_send(2, 0, "a")
    z_send(6, HALF, "b")
    second_done(1)
    first_near(1)
    second_near(0)
    z_send(1, HALF, "a")
    z_send(7, 0, "b")
    second_done(3)
    first_near(3)
    stat_send(3, stat_sum(2))
    z_send(1, 0, "a")
    z_send(7, HALF, "b")
    second_done(0)
    text_last()
    everyone = stat_sum(3)
    share = 1.0 / float(PAIRS * PAIRS)
    stats_out[0] = jnp.sum(everyone[0:1, :]) * share
    stats_out[1] = jnp.sum(everyone[1:2, :] * warmth) * share
    stats_out[2] = jnp.sum(everyone[2:3, :]) * share
    image_last()
    all_sent(
        {
            "text": text,
            "image": image,
            "label": labels.at[0],
            "labels": labels,
            "sum": coded_out,
            "stat": stat_slots,
        }
    )


def on_device(picture, caption, labels, warmth, offset):
    vmem = pl.BlockSpec(memory_space=pltpu.VMEM)
    smem = pl.BlockSpec(memory_space=pltpu.SMEM)
    hbm = pl.BlockSpec(memory_space=pl.ANY)
    grad = jax.ShapeDtypeStruct((ROWS, D), jnp.float32)
    return pl.pallas_call(
        kernel,
        out_shape=(grad, grad, jax.ShapeDtypeStruct((3,), jnp.float32)),
        in_specs=[smem, smem, vmem, hbm, hbm],
        out_specs=(vmem, vmem, smem),
        scratch_shapes=[
            pltpu.VMEM((TILE, D), jnp.bfloat16),
            pltpu.VMEM((TILE, D), jnp.bfloat16),
            pltpu.VMEM((2, NZ, 8, LANES), jnp.int32),
            pltpu.VMEM((8, TILE), jnp.int32),
            pltpu.VMEM((2, 256, TILE), jnp.float32),
            pltpu.VMEM((TILE, TILE), jnp.bfloat16),
            pltpu.VMEM((TILE, D), jnp.float32),
            pltpu.VMEM((TILE, D), jnp.float32),
            pltpu.VMEM((TILE // HALF, QUARTER, LANES), jnp.float32),
            pltpu.VMEM((TILE // HALF, QUARTER, LANES), jnp.float32),
            pltpu.VMEM((N_TILES, QUARTER, LANES), jnp.int16),
            pltpu.VMEM((N_TILES, QUARTER, LANES), jnp.int16),
            pltpu.VMEM((3, 8, LANES), jnp.float32),
            pltpu.VMEM((2 + NX + NY + NZ, 8, LANES), jnp.float32),
            pltpu.SemaphoreType.DMA((2,)),
            pltpu.SemaphoreType.DMA((N_SEND,)),
            pltpu.SemaphoreType.DMA((N_RECV,)),
        ],
        compiler_params=pltpu.CompilerParams(
            collective_id=0, has_side_effects=True, vmem_limit_bytes=56 << 20
        ),
    )(warmth, offset, labels.reshape(4, LANES), picture, caption)


def solution(mesh):
    rows = P(("grp", "mem"), None)
    return jax.shard_map(
        on_device,
        mesh=mesh,
        in_specs=(rows, rows, P("grp"), P(), P()),
        out_specs=(rows, rows, P()),
        check_vma=False,
    )
```

time: 319 us -> 64.5 us (0.20)
  waiting for transfers between devices: 186 us -> 0 us
  blocking collectives: 84.3 us -> 0 us
  Pallas kernels: 0 us -> 58.6 us
  matrix products: 25.3 us -> 0 us
  between operations: 15.1 us -> 1.94 us
  other arithmetic: 5.83 us -> 0 us
    all_gather x2 -> x0, waiting for transfers between devices: 110 us -> none  [the longest x1 69.4 us: on_device(): segment_part = lax.all_gather(caption_vectors, 'grp', axis=0, tiled=True)]
    psum x1 -> x0, blocking collectives: 84.3 us -> none  [on_device(): totals = lax.psum(stat_sums, ('grp', 'mem'))]
    reduce_scatter x2 -> x0, waiting for transfers between devices: 74.2 us -> none  [the longest x1 74.2 us: on_device(): lax.psum_scatter(text_acc, 'grp', scatter_dimension=0, tiled=True)]
    pallas_call x0 -> x1, Pallas kernels: none -> 58.6 us  [on_device(): pl.pallas_call(kernel, out_shape=(grad, grad, jax.ShapeDtypeStruct((3,),...]
    dot_general x3 -> x0, matrix products: 25.3 us -> none  [the longest x1 10.1 us: score_tile(): lax.dot_general(images_in_group, segment_part, (((1,), (1,)), ((), ())),...]
    mul x2 -> x0, other arithmetic: 3.39 us -> none  [the longest x1 1.7 us: on_device(): image_grad = image_total * stretch_factor]
  transfers between devices with their start and end apart: 4 -> 0, of which waited for: 3 -> 0; matrix products, arithmetic and copies ran while one was open for 4% -> 0% of each run, Pallas kernels for 0% -> 0%
where the time goes in v2:
time: 64.5 us; the launch traced here: 63.5 us
  Pallas kernels  58.6 us (91%)
  local copies, waits for them, and re-layouts  2.97 us (5%)
  between operations  1.94 us (3%)
    pallas_call x1, Pallas kernels, on_device(): pl.pallas_call(kernel, out_shape=(grad, grad, jax.ShapeDtypeStruct((3,),...  58.6 us
    unnamed x7, local copies, waits for them, and re-layouts  2.97 us

profile of v2, /device:TPU:1, one launch (start us, length us, event | category | flops | bytes accessed | tf_op | source)
XLA Modules:
  0.0 63.5 jit_solution(634804950256119165)
XLA Ops:
  1.9 58.6 %shard_map.76 = (f32[64,1152]{1,0:T(8,128)}, f32[64,1152]{1,0:T(8,128)}, f32[3]{0:T(128)}) custom-call(f32[1]{0:T(128)S(6)} %copy.11.warmth_ref, f32[1]{0:T(128)S(6)} %copy.12.offset_ref, s32[4,128]{1,0:T(4,128)} %bitcast.1, bf16[64,1152]{1,0:T(8,128)(2,1)} %image_hbm.1, bf16[64,1152]{1,0:T(8,128)(2,1)} %text_hbm.1), custom_call_target="tpu_custom_call" | custom-call | tf_op jit(solution)/shard_map/pallas_call | solution.py:593
  60.5 0.0 copy-start
  60.5 1.7 %copy.13 = f32[64,1152]{1,0:T(8,128)} copy(f32[64,1152]{1,0:T(8,128)} %get-tuple-element.6) | data formatting | bytes 589824
  62.2 0.0 copy-done
  62.2 0.0 copy-start.1
  62.2 0.7 %copy.14 = f32[64,1152]{1,0:T(8,128)} copy(f32[64,1152]{1,0:T(8,128)S(1)} %copy-done) | data formatting | bytes 589824
  63.0 0.0 copy-done.1
  63.0 0.5 copy.15
Async XLA Ops:
  60.5 1.8 %copy-start = (f32[64,1152]{1,0:T(8,128)S(1)}, f32[64,1152]{1,0:T(8,128)}, u32[]{:S(2)}) copy-start(f32[64,1152]{1,0:T(8,128)} %get-tuple-element.7) | copy-start | bytes 884740
  62.2 0.7 %copy-start.1 = (f32[3]{0:T(128)S(1)}, f32[3]{0:T(128)}, u32[]{:S(2)}) copy-start(f32[3]{0:T(128)} %get-tuple-element.8) | copy-start | bytes 40

commit v3 on v2

v3 whole, which is shorter than its diff:
```python
import jax
import jax.numpy as jnp
from jax import lax
from jax.experimental import pallas as pl
from jax.experimental.pallas import tpu as pltpu
from jax.sharding import PartitionSpec as P

MESH = pl.DeviceIdType.MESH
NX, NY, NZ = 4, 4, 8
ROWS = 64
HALF, QUARTER = 32, 16
D = 1152
LANES = 128
WIDE = D // LANES
TILE = 1024
PAIRS = 16384
LEVELS = 32000.0
SMALLEST = 1e-30

FAR_FIRST = (2, 1, 3, 0)
TEXT_HALVES = [
    (h, i, j)
    for i in FAR_FIRST
    for h in (0, 1)
    for j in (FAR_FIRST if h == 0 else FAR_FIRST[::-1])
]
TEXT_AT = {key: n * HALF for n, key in enumerate(TEXT_HALVES)}
PARTS = ((4, 3), (5, 2), (6, 1), (7, 0))
IMAGE_ORDER = [(c, d) for part in PARTS for c in (1, 0) for d in part]
IMAGE_AT = {key: n * ROWS for n, key in enumerate(IMAGE_ORDER)}
N_SEND, N_RECV = 6, 126
N_TILES = 1152
ORDER = [
    "begin", ("z", 7, 0), ("z", 1, 48), ("t", 0, 3, 0), ("t", 0, 1, 0), ("t", 1, 3, 0), ("t", 1, 1, 0),
    ("z", 1, 32), ("z", 7, 16), ("z", 7, 32), ("z", 1, 16), ("z", 7, 48), ("z", 1, 0), ("t", 0, 2, 0),
    ("t", 1, 2, 0), ("t", 1, 0, 3), ("t", 1, 0, 1), "label", ("c", 3), ("z", 2, 48), ("z", 6, 0),
    ("t", 0, 0, 3), ("t", 0, 0, 1), ("z", 2, 32), ("z", 6, 16), "labels", ("t", 1, 3, 3), ("t", 0, 3, 3),
    ("t", 0, 3, 1), ("z", 2, 16), ("t", 1, 3, 1), ("z", 6, 32), ("z", 2, 0), ("z", 6, 48), ("t", 1, 1, 3),
    ("t", 1, 1, 1), ("t", 0, 1, 1), ("t", 0, 1, 3), ("z", 3, 48), ("z", 5, 0), ("c", 2), ("t", 1, 2, 3),
    ("t", 1, 2, 1), ("t", 0, 2, 3), ("t", 0, 2, 1), ("z", 3, 32), ("z", 5, 16), ("z", 3, 16), ("z", 5, 32),
    ("z", 3, 0), ("z", 5, 48), ("t", 1, 2, 2), ("t", 1, 0, 2), ("t", 0, 2, 2), ("p", 0, 1), ("t", 0, 0, 2),
    ("p", 3, 1), ("c", 1), ("t", 0, 3, 2), ("t", 1, 3, 2), ("p", 2, 1), ("t", 1, 1, 2), ("z", 4, 48),
    ("z", 4, 32), ("z", 4, 0), ("z", 4, 16), ("t", 0, 1, 2), ("p", 1, 1), ("I", 2), ("c", 0), ("p", 1, 0),
    ("p", 0, 0), ("p", 2, 0), ("p", 3, 0), ("s", 0), ("T", 1), ("sf", 1), ("I", 0), ("co", 0), ("T", 0),
    ("sf", 2), ("cw", 4), ("zs", 4, 16), ("zs", 4, 0), ("cw", 3), ("I", 1), ("s", 1), ("co", 1), ("T", 2),
    ("sf", 3), ("cw", 5), ("zs", 3, 32), ("zs", 3, 16), ("zs", 3, 48), ("sn", 2), ("zs", 3, 0), ("sn", 1),
    ("cw", 2), ("co", 2), ("T", 3), ("sf", 0), ("s", 2), ("cw", 6), ("zs", 2, 32), ("sn", 3), ("zs", 2, 16),
    ("I", 3), ("zs", 2, 48), ("zs", 2, 0), ("co", 3), ("cw", 1), ("sn", 0), ("f", 2), ("f", 1), ("cw", 7),
    ("zs", 1, 32), ("zs", 1, 16), ("cw", 0), ("s", 3), ("zs", 1, 48), ("f", 3), ("zs", 1, 0), ("zl", 16),
    ("zl", 32), ("zl", 0), ("zl", 48), ("tl", 1), ("tl", 0), ("s", 4),
]


def fold(values):
    rows, columns = values.shape
    parts = [
        values[r : r + 8, c : c + LANES]
        for r in range(0, rows, 8)
        for c in range(0, columns, LANES)
    ]
    while len(parts) > 1:
        parts = [a + b for a, b in zip(parts[::2], parts[1::2], strict=True)]
    return parts[0]


def kernel(
    warmth_hbm,
    offset_hbm,
    labels_ref,
    image_hbm,
    text_hbm,
    image_out,
    text_out,
    stats_out,
    image,
    text,
    labels,
    label_row,
    scores,
    coef,
    image_sum,
    text_sum,
    image_top,
    text_top,
    coded_out,
    coded_in,
    stats,
    stat_slots,
    warmth_ref,
    offset_ref,
    local_sem,
    send_sem,
    recv_sem,
):
    group, member = lax.axis_index("grp"), lax.axis_index("mem")
    core, x, z_high = lax.rem(group, 2), lax.rem(group // 2, NX), group // (2 * NX)
    y, z_low = lax.rem(member, NY), member // NY
    z = z_high * 2 + z_low

    def device(dx=0, dy=0, dz=0, dc=0):
        to_x, to_y = lax.rem(x + dx + NX, NX), lax.rem(y + dy + NY, NY)
        to_z, to_c = lax.rem(z + dz + NZ, NZ), lax.rem(core + dc, 2)
        return ((to_z // 2 * NX + to_x) * 2 + to_c, lax.rem(to_z, 2) * NY + to_y)

    ahead = {"x": device(dx=1), "y": device(dy=1), "z": device(dz=1)}
    behind = {"x": device(dx=-1), "y": device(dy=-1), "z": device(dz=-1)}
    beyond = {"x": device(dx=2), "y": device(dy=2)}
    other = device(dc=1)

    own_image = pltpu.make_async_copy(
        image_hbm, image.at[pl.ds(IMAGE_AT[0, 0], ROWS)], local_sem.at[0]
    )
    own_text = pltpu.make_async_copy(
        text_hbm, text.at[pl.ds(TEXT_AT[0, 0, 0], ROWS)], local_sem.at[1]
    )
    scalars = [
        pltpu.make_async_copy(warmth_hbm, warmth_ref, local_sem.at[2]),
        pltpu.make_async_copy(offset_hbm, offset_ref, local_sem.at[3]),
    ]
    own_image.start()
    own_text.start()
    for copy in scalars:
        copy.start()

    partners = [other]
    partners += [device(dx=d) for d in range(1, NX)]
    partners += [device(dy=d) for d in range(1, NY)]
    partners += [device(dz=d) for d in range(1, NZ)]
    barrier = pltpu.get_barrier_semaphore()
    for partner in partners:
        pl.semaphore_signal(barrier, inc=1, device_id=partner, device_id_type=MESH)
    pl.semaphore_wait(barrier, len(partners))

    recv_of, sent_of = {}, {}

    def place(key):
        return recv_sem.at[recv_of.setdefault(key, len(recv_of))]

    def send(kind, amount, source, target, to, key):
        at = list(sent_of).index(kind) if kind in sent_of else len(sent_of)
        sent_of[kind] = sent_of.get(kind, 0) + amount
        pltpu.make_async_remote_copy(
            src_ref=source,
            dst_ref=target,
            send_sem=send_sem.at[at],
            recv_sem=place(key),
            device_id=to,
            device_id_type=MESH,
        ).start()

    def expect(key, ref):
        pltpu.make_async_remote_copy(
            src_ref=ref,
            dst_ref=ref,
            send_sem=send_sem.at[0],
            recv_sem=place(key),
            device_id=other,
            device_id_type=MESH,
        ).wait_recv()

    def all_sent(refs):
        for at, (kind, amount) in enumerate(sent_of.items()):
            ref = refs[kind].at[pl.ds(0, amount)]
            pltpu.make_async_remote_copy(
                src_ref=ref,
                dst_ref=ref,
                send_sem=send_sem.at[at],
                recv_sem=recv_sem.at[0],
                device_id=other,
                device_id_type=MESH,
            ).wait_send()

    def axis_of(h, nth):
        return "xy"[(h + nth) % 2]

    tasks = {}

    def send_text(h, i, j, row, rows, nth, step):
        there = (h, (i - step) % 4, j) if nth == 0 else (h, i, (j - step) % 4)
        send(
            "text",
            rows,
            text.at[pl.ds(TEXT_AT[h, i, j] + row, rows)],
            text.at[pl.ds(TEXT_AT[there] + row, rows)],
            {1: ahead, -1: behind, 2: beyond}[step][axis_of(h, nth)],
            ("text", *there),
        )

    def spread(h, i, j, nth):
        send_text(h, i, j, 0, HALF, nth, 1)
        send_text(h, i, j, 0, HALF, nth, -1)

    def on_text(h, i, j):
        expect(("text", h, i, j), text.at[pl.ds(0, HALF)])
        if j == 0:
            spread(h, i, j, 1)
            if i == 2:
                send_text(h, i, j, 0, HALF, 1, 2)
        elif j == 3 and i != 2:
            send_text(h, i, j, 0, QUARTER, 1, 1)
        elif j == 1 and i != 2:
            send_text(h, i, j, QUARTER, QUARTER, 1, -1)

    for h in (0, 1):
        for i in range(4):
            for j in range(4):
                if i or j:
                    tasks["t", h, i, j] = lambda a=(h, i, j): on_text(*a)

    def send_image(d, row, rows, to, there, key):
        send(
            "image",
            rows,
            image.at[pl.ds(IMAGE_AT[0, d] + row, rows)],
            image.at[pl.ds(IMAGE_AT[there] + row, rows)],
            to,
            key,
        )

    def across(d, row, rows):
        part = next(n for n, p in enumerate(PARTS) if d in p)
        send_image(d, row, rows, other, (1, d), ("across", part))

    def along_z(d, row, step):
        there = (d - step) % NZ
        to = (ahead if step == 1 else behind)["z"]
        send_image(d, row, QUARTER, to, (0, there), ("z", there, row))

    def on_image(d, row):
        expect(("z", d, row), image.at[pl.ds(0, QUARTER)])
        if d > 5 or (d == 5 and row < HALF):
            along_z(d, row, 1)
        if d < 3 or (d == 3 and row >= HALF):
            along_z(d, row, -1)
        if row % HALF == (QUARTER if d >= 4 and not (d == 4 and row >= HALF) else 0):
            across(d, row - row % HALF, HALF)

    for d in range(1, NZ):
        for row in range(0, ROWS, QUARTER):
            tasks["z", d, row] = lambda a=(d, row): on_image(*a)
    for n in range(len(PARTS)):
        tasks["c", n] = lambda n=n: expect(
            ("across", n), image.at[pl.ds(0, ROWS * 2)]
        )

    def begin():
        own_text.wait()
        for h in (0, 1):
            spread(h, 0, 0, 0)
        own_image.wait()
        for row in range(0, ROWS, QUARTER):
            along_z(0, row, 1)
            along_z(0, ROWS - QUARTER - row, -1)
        for h in (0, 1):
            send_text(h, 0, 0, 0, HALF, 0, 2)
        for h in (0, 1):
            spread(h, 0, 0, 1)
        across(0, 0, ROWS)
        mine = jnp.broadcast_to(labels_ref[pl.ds(member // 2, 1), :], (8, LANES))
        turned = pltpu.roll(mine, ROWS, 1)
        in_upper = jnp.broadcast_to(lax.rem(member, 2), (8, LANES)) == 1
        labels[0, 0] = jnp.where((lane >= ROWS) == in_upper, mine, turned)
        for d in range(1, NZ):
            there = labels.at[0, NZ - d]
            send("label", 1, labels.at[0, 0], there, device(dz=d), "label")
        for n in range(3):
            stats[n] = zero

    def on_label():
        expect("label", labels.at[0, pl.ds(1, NZ - 1)])
        here, there = labels.at[pl.ds(0, 1)], labels.at[pl.ds(1, 1)]
        send("labels", 1, here, there, other, "labels")

    def on_labels():
        expect("labels", labels.at[pl.ds(0, 1)])
        for at in range(0, TILE // ROWS, 2):
            label_row[:, at * ROWS : (at + 2) * ROWS] = jnp.where(
                lane < ROWS, labels[IMAGE_ORDER[at]], labels[IMAGE_ORDER[at + 1]]
            )

    for copy in scalars:
        copy.wait()
    lane = lax.broadcasted_iota(jnp.int32, (8, LANES), 1)
    zero = jnp.zeros((8, LANES), jnp.float32)
    warmth = jnp.exp(jnp.full((1, 1), warmth_ref[0], jnp.float32))
    offset = offset_ref[0]
    stretch = warmth * (1.0 / PAIRS)
    tasks["begin"] = begin
    tasks["label"] = on_label
    tasks["labels"] = on_labels

    def pairs(chunk, side):
        first, left = chunk * 256, side * 512
        slot = (chunk + side) % 2
        scores[slot] = lax.dot_general(
            text[pl.ds(first, 256), :],
            image[pl.ds(left, 512), :],
            (((1,), (1,)), ((), ())),
            preferred_element_type=jnp.float32,
        )
        for row in range(0, 256, HALF):
            h, i, j = TEXT_HALVES[(first + row) // HALF]
            rx, ry = (i, j) if h == 0 else (j, i)
            owner_x, owner_y = lax.rem(x + rx, NX), lax.rem(y + ry, NY)
            base = (
                ((z_high * NX + owner_x) * 2 + core) * 8 + z_low * NY + owner_y
            ) * ROWS + h * HALF
            position = lax.broadcasted_iota(jnp.int32, (HALF, 1), 0) + base
            for column in (0, 256):
                s = scores[slot, pl.ds(row, HALF), pl.ds(column, 256)]
                logit = s * warmth + offset
                matched = label_row[0:1, pl.ds(left + column, 256)] == position
                signed = jnp.where(matched, -logit, logit)
                e = jnp.exp(-jnp.abs(signed))
                one_e = 1.0 + e
                inverse = 1.0 / one_e
                chance = jnp.where(signed >= 0, inverse, e * inverse)
                factor = jnp.where(matched, -chance, chance)
                coef[pl.ds(first + row, HALF), pl.ds(left + column, 256)] = factor.astype(
                    jnp.bfloat16
                )
                grown = zero
                for r in range(0, HALF, 8):
                    for c in range(0, 256, LANES):
                        piece = slice(r, r + 8), slice(c, c + LANES)
                        grown = grown * one_e[piece] + e[piece]
                stats[0] += fold(jnp.maximum(signed, 0.0)) + jnp.log1p(grown)
                stats[1] += fold(factor * s)
                stats[2] += fold(factor)

    def find_tops(sums, tops, first):
        for row in range(first, first + 256, HALF):
            top = None
            for r in range(0, HALF, 8):
                for c in range(0, D, LANES):
                    part = jnp.abs(sums[pl.ds(row + r, 8), c : c + LANES])
                    top = part if top is None else jnp.maximum(top, part)
            top = jnp.max(jnp.max(top, axis=1, keepdims=True), axis=0, keepdims=True)
            power = jnp.ceil(jnp.log2(jnp.maximum(top, SMALLEST)))
            tops[row // HALF] = jnp.broadcast_to(power, (QUARTER, LANES))

    def text_part(chunk):
        at = pl.ds(chunk * 256, 256)
        text_sum[at, :] = jnp.dot(
            coef[at, :], image[...], preferred_element_type=jnp.float32
        )
        find_tops(text_sum, text_top, chunk * 256)

    def image_part(chunk):
        at = pl.ds(chunk * 256, 256)
        image_sum[at, :] = lax.dot_general(
            coef[:, at],
            text[...],
            (((0,), (0,)), ((), ())),
            preferred_element_type=jnp.float32,
        )
        find_tops(image_sum, image_top, chunk * 256)

    messages = {}
    used = [0]

    def arrived(parts):
        found = {}
        for adds in parts:
            for name, _ in adds:
                if name not in found:
                    power = coded_in[messages[name]].astype(jnp.float32)
                    found[name] = jnp.exp2(power) * (1.0 / LEVELS), power
        return found

    def summed(sums, row, wide, adds, found):
        value = sums[pl.ds(row, QUARTER), wide * LANES : (wide + 1) * LANES]
        for name, nth in adds:
            tile = coded_in[messages[name] + 1 + nth * WIDE + wide]
            value = value + tile.astype(jnp.float32) * found[name][0]
        return value

    def send_sums(*sending):
        ready = []
        for name, sums, tops, row, parts, to, key in sending:
            start, count = used[0], 1 + len(parts) * WIDE
            messages[name] = start
            used[0] += count
            found = arrived(parts)
            powers = [tops[row // HALF]]
            if len(parts) * QUARTER > HALF:
                powers[0] = jnp.maximum(powers[0], tops[row // HALF + 1])
            powers += [power for _, power in found.values()]
            while len(powers) > 1:
                powers = powers[2:] + [jnp.maximum(powers[0], powers[1]) + 1.0]
            coded_out[start] = powers[0].astype(jnp.int16)
            scale = jnp.exp2(-powers[0]) * LEVELS
            for n, adds in enumerate(parts):
                for wide in range(WIDE):
                    value = summed(sums, row + n * QUARTER, wide, adds, found)
                    coded_out[start + 1 + n * WIDE + wide] = (
                        jnp.round(value * scale).astype(jnp.int32).astype(jnp.int16)
                    )
            ready.append((pl.ds(start, count), count, to, key))
        for at, count, to, key in ready:
            send("sum", count, coded_out.at[at], coded_in.at[at], to, key)

    def await_sum(key, *sizes):
        count = sum(1 + rows // QUARTER * WIDE for rows in sizes)
        expect(key, coded_in.at[pl.ds(0, count)])

    def direct(i):
        return i == 0

    def second_far(i):
        sending = []
        for h in (0, 1):
            axis, at = axis_of(h, 1), TEXT_AT[h, i, 2]
            if direct(i):
                name, to = (h, i, "far"), beyond[axis]
                sending.append(
                    (name, text_sum, text_top, at, [[], []], to, (h, i, "n"))
                )
                continue
            for far, row, to in (("fa", 0, ahead), ("fb", QUARTER, behind)):
                name = (h, i, far)
                sending.append(
                    (name, text_sum, text_top, at + row, [[]], to[axis], name)
                )
        send_sums(*sending)

    def second_near(i):
        sending = []
        for h in (0, 1):
            for j, far, near, to in ((1, "fa", "na", ahead), (3, "fb", "nb", behind)):
                parts = [[], []]
                if not direct(i):
                    await_sum((h, i, far), QUARTER)
                    parts[j == 3].append(((h, i, far), 0))
                at, to = TEXT_AT[h, i, j], to[axis_of(h, 1)]
                name = (h, i, near)
                sending.append((name, text_sum, text_top, at, parts, to, (h, i, "n")))
        send_sums(*sending)

    def line(h, i, nth):
        adds = [((h, i, "na"), nth), ((h, i, "nb"), nth)]
        return adds + [((h, i, "far"), nth)] if direct(i) else adds

    def first(i):
        sending = []
        for h in (0, 1):
            await_sum((h, i, "n"), *[HALF] * (3 if direct(i) else 2))
            to = {1: ahead, 2: beyond, 3: behind}[i][axis_of(h, 0)]
            parts = [line(h, i, 0), line(h, i, 1)]
            at = TEXT_AT[h, i, 0]
            sending.append(((h, "n", i), text_sum, text_top, at, parts, to, (h, "n")))
        send_sums(*sending)

    def text_last(h):
        await_sum((h, 0, "n"), *[HALF] * (3 if direct(0) else 2))
        await_sum((h, "n"), HALF, HALF, HALF)
        for n in (0, 1):
            adds = line(h, 0, n) + [((h, "n", i), n) for i in (1, 2, 3)]
            found = arrived([adds])
            at = h * HALF + n * QUARTER
            row = TEXT_AT[h, 0, 0] + n * QUARTER
            for wide in range(WIDE):
                value = summed(text_sum, row, wide, adds, found)
                text_out[at : at + QUARTER, wide * LANES : (wide + 1) * LANES] = (
                    value * stretch
                )

    for i in range(4):
        tasks["sf", i] = lambda i=i: second_far(i)
        tasks["sn", i] = lambda i=i: second_near(i)
        if i:
            tasks["f", i] = lambda i=i: first(i)
    for h in (0, 1):
        tasks["tl", h] = lambda h=h: text_last(h)

    def to_other(n):
        sending = []
        for d in PARTS[n]:
            parts = [[] for _ in range(4)]
            at = IMAGE_AT[1, d]
            sending.append((("c", d), image_sum, image_top, at, parts, other, ("c", d)))
        send_sums(*sending)

    def z_adds(d, row):
        adds = [(("c", d), row // QUARTER)]
        if d < 4 and (d < 3 or row < HALF):
            adds.append((("za", d + 1, row), 0))
        if (d > 4 or d == 0) and (d != 5 or row >= HALF):
            adds.append((("zb", (d - 1) % NZ, row), 0))
        return adds

    def z_send(far, row):
        sending = []
        for d, r, way, to in (
            (far, row, "za", ahead),
            (NZ - far, ROWS - QUARTER - row, "zb", behind),
        ):
            adds = z_adds(d, r)
            for name, _ in adds[1:]:
                await_sum(name, QUARTER)
            name, at = (way, d, r), IMAGE_AT[0, d] + r
            sending.append((name, image_sum, image_top, at, [adds], to["z"], name))
        send_sums(*sending)

    def image_last(row):
        adds = z_adds(0, row)
        for name, _ in adds[1:]:
            await_sum(name, QUARTER)
        found = arrived([adds])
        for wide in range(WIDE):
            value = summed(image_sum, IMAGE_AT[0, 0] + row, wide, adds, found)
            image_out[row : row + QUARTER, wide * LANES : (wide + 1) * LANES] = (
                value * stretch
            )

    for n in range(4):
        tasks["co", n] = lambda n=n: to_other(n)
        tasks["T", n] = lambda n=n: text_part(n)
        tasks["I", n] = lambda n=n: image_part(n)
        for chunk in range(4):
            if n < 2:
                tasks["p", chunk, n] = lambda a=(chunk, n): pairs(*a)
    for d in range(NZ):
        tasks["cw", d] = lambda d=d: await_sum(("c", d), ROWS)
        for row in range(0, ROWS, QUARTER):
            if d == 0:
                tasks["zl", row] = lambda row=row: image_last(row)
            elif d < 4 or (d == 4 and row < HALF):
                tasks["zs", d, row] = lambda a=(d, row): z_send(*a)

    stat_axes = (
        (2, core, lambda d: device(dc=d)),
        (NX, x, lambda d: device(dx=d)),
        (NY, y, lambda d: device(dy=d)),
        (NZ, z, lambda d: device(dz=d)),
    )

    def stat_send(nth, value):
        base = sum(a[0] for a in stat_axes[:nth])
        size, me, to = stat_axes[nth]
        stat_slots[base + me] = value
        for d in range(1, size):
            slot = stat_slots.at[pl.ds(base + me, 1)]
            send("stat", 1, slot, slot, to(d), ("stat", nth))

    def stat_sum(nth):
        base, size = sum(a[0] for a in stat_axes[:nth]), stat_axes[nth][0]
        expect(("stat", nth), stat_slots.at[pl.ds(0, size - 1)])
        value = stat_slots[base]
        for n in range(1, size):
            value = value + stat_slots[base + n]
        return value

    def first_stats():
        rows = [jnp.sum(stats[n], axis=0, keepdims=True) for n in range(3)]
        rows.append(jnp.zeros((5, LANES), jnp.float32))
        stat_send(0, jnp.concatenate(rows, axis=0))

    def last_stats():
        everyone = stat_sum(3)
        share = 1.0 / float(PAIRS * PAIRS)
        stats_out[0] = jnp.sum(everyone[0:1, :]) * share
        stats_out[1] = jnp.sum(everyone[1:2, :] * warmth) * share
        stats_out[2] = jnp.sum(everyone[2:3, :]) * share

    tasks["s", 0] = first_stats
    for n in (1, 2, 3):
        tasks["s", n] = lambda n=n: stat_send(n, stat_sum(n - 1))
    tasks["s", 4] = last_stats

    for task in ORDER:
        tasks[task]()
    all_sent(
        {
            "text": text,
            "image": image,
            "label": labels.at[0],
            "labels": labels,
            "sum": coded_out,
            "stat": stat_slots,
        }
    )


def on_device(picture, caption, labels, warmth, offset):
    vmem = pl.BlockSpec(memory_space=pltpu.VMEM)
    smem = pl.BlockSpec(memory_space=pltpu.SMEM)
    hbm = pl.BlockSpec(memory_space=pl.ANY)
    grad = pltpu.VMEM((ROWS, D), jnp.float32)
    return pl.pallas_call(
        kernel,
        out_shape=(grad, grad, jax.ShapeDtypeStruct((3,), jnp.float32)),
        in_specs=[hbm, hbm, vmem, hbm, hbm],
        out_specs=(vmem, vmem, smem),
        scratch_shapes=[
            pltpu.VMEM((TILE, D), jnp.bfloat16),
            pltpu.VMEM((TILE, D), jnp.bfloat16),
            pltpu.VMEM((2, NZ, 8, LANES), jnp.int32),
            pltpu.VMEM((8, TILE), jnp.int32),
            pltpu.VMEM((2, 256, 512), jnp.float32),
            pltpu.VMEM((TILE, TILE), jnp.bfloat16),
            pltpu.VMEM((TILE, D), jnp.float32),
            pltpu.VMEM((TILE, D), jnp.float32),
            pltpu.VMEM((TILE // HALF, QUARTER, LANES), jnp.float32),
            pltpu.VMEM((TILE // HALF, QUARTER, LANES), jnp.float32),
            pltpu.VMEM((N_TILES, QUARTER, LANES), jnp.int16),
            pltpu.VMEM((N_TILES, QUARTER, LANES), jnp.int16),
            pltpu.VMEM((3, 8, LANES), jnp.float32),
            pltpu.VMEM((2 + NX + NY + NZ, 8, LANES), jnp.float32),
            pltpu.SMEM((1,), jnp.float32),
            pltpu.SMEM((1,), jnp.float32),
            pltpu.SemaphoreType.DMA((4,)),
            pltpu.SemaphoreType.DMA((N_SEND,)),
            pltpu.SemaphoreType.DMA((N_RECV,)),
        ],
        compiler_params=pltpu.CompilerParams(
            collective_id=0, has_side_effects=True, vmem_limit_bytes=56 << 20
        ),
    )(warmth, offset, labels.reshape(4, LANES), picture, caption)


def solution(mesh):
    rows = P(("grp", "mem"), None)
    return jax.shard_map(
        on_device,
        mesh=mesh,
        in_specs=(rows, rows, P("grp"), P(), P()),
        out_specs=(rows, rows, P()),
        check_vma=False,
    )
```

time: 64.5 us -> 59.5 us (0.922); the launches traced: 63.5 us -> 59.3 us
  Pallas kernels: 58.6 us -> 55.5 us
  local copies, waits for them, and re-layouts: 2.97 us -> 1.94 us
    pallas_call x1, Pallas kernels: 58.6 us -> 55.5 us  [on_device(): pl.pallas_call(kernel, out_shape=(grad, grad, jax.ShapeDtypeStruct((3,),...]
    unnamed x7 -> x5, local copies, waits for them, and re-layouts: 2.97 us -> 1.94 us
where the time goes in v3:
time: 59.5 us; the launch traced here: 59.3 us
  Pallas kernels  55.5 us (93%)
  local copies, waits for them, and re-layouts  1.94 us (3%)
  between operations  1.93 us (3%)
    pallas_call x1, Pallas kernels, on_device(): pl.pallas_call(kernel, out_shape=(grad, grad, jax.ShapeDtypeStruct((3,),...  55.5 us
    unnamed x5, local copies, waits for them, and re-layouts  1.94 us

profile of v3, /device:TPU:1, one launch (start us, length us, event | category | flops | bytes accessed | tf_op | source)
XLA Modules:
  0.0 59.3 jit_solution(12993236407811497971)
XLA Ops:
  1.9 55.5 %shard_map.76 = (f32[64,1152]{1,0:T(8,128)S(1)}, f32[64,1152]{1,0:T(8,128)S(1)}, f32[3]{0:T(128)}) custom-call(f32[1]{0:T(128)S(6)} %copy.13.warmth_hbm, f32[1]{0:T(128)S(6)} %copy.14.offset_hbm, s32[4,128]{1,0:T(4,128)} %bitcast.1, bf16[64,1152]{1,0:T(8,128)(2,1)} %image_hbm.1, bf16[64,1152]{1,0:T(8,128)(2,1)} %text_hbm.1), custom_call_target="tpu_custom_call" | custom-call | tf_op jit(solution)/shard_map/pallas_call | solution.py:590
  57.4 0.7 %copy.11 = f32[64,1152]{1,0:T(8,128)} copy(f32[64,1152]{1,0:T(8,128)S(1)} %get-tuple-element.3) | data formatting | bytes 589824
  58.1 0.0 copy-start
  58.1 0.7 %copy.12 = f32[64,1152]{1,0:T(8,128)} copy(f32[64,1152]{1,0:T(8,128)S(1)} %get-tuple-element.4) | data formatting | bytes 589824
  58.8 0.0 copy-done
  58.8 0.5 copy.15
Async XLA Ops:
  58.1 0.7 %copy-start = (f32[3]{0:T(128)S(1)}, f32[3]{0:T(128)}, u32[]{:S(2)}) copy-start(f32[3]{0:T(128)} %get-tuple-element.11) | copy-start | bytes 40

commit v4 on v3

--- a/solution.py
+++ b/solution.py
@@ -28,26 +28,28 @@
 PARTS = ((4, 3), (5, 2), (6, 1), (7, 0))
 IMAGE_ORDER = [(c, d) for part in PARTS for c in (1, 0) for d in part]
 IMAGE_AT = {key: n * ROWS for n, key in enumerate(IMAGE_ORDER)}
-N_SEND, N_RECV = 6, 126
+N_SEND, N_RECV = 6, 128
 N_TILES = 1152
 ORDER = [
-    "begin", ("z", 7, 0), ("z", 1, 48), ("t", 0, 3, 0), ("t", 0, 1, 0), ("t", 1, 3, 0), ("t", 1, 1, 0),
-    ("z", 1, 32), ("z", 7, 16), ("z", 7, 32), ("z", 1, 16), ("z", 7, 48), ("z", 1, 0), ("t", 0, 2, 0),
-    ("t", 1, 2, 0), ("t", 1, 0, 3), ("t", 1, 0, 1), "label", ("c", 3), ("z", 2, 48), ("z", 6, 0),
-    ("t", 0, 0, 3), ("t", 0, 0, 1), ("z", 2, 32), ("z", 6, 16), "labels", ("t", 1, 3, 3), ("t", 0, 3, 3),
-    ("t", 0, 3, 1), ("z", 2, 16), ("t", 1, 3, 1), ("z", 6, 32), ("z", 2, 0), ("z", 6, 48), ("t", 1, 1, 3),
-    ("t", 1, 1, 1), ("t", 0, 1, 1), ("t", 0, 1, 3), ("z", 3, 48), ("z", 5, 0), ("c", 2), ("t", 1, 2, 3),
-    ("t", 1, 2, 1), ("t", 0, 2, 3), ("t", 0, 2, 1), ("z", 3, 32), ("z", 5, 16), ("z", 3, 16), ("z", 5, 32),
-    ("z", 3, 0), ("z", 5, 48), ("t", 1, 2, 2), ("t", 1, 0, 2), ("t", 0, 2, 2), ("p", 0, 1), ("t", 0, 0, 2),
-    ("p", 3, 1), ("c", 1), ("t", 0, 3, 2), ("t", 1, 3, 2), ("p", 2, 1), ("t", 1, 1, 2), ("z", 4, 48),
-    ("z", 4, 32), ("z", 4, 0), ("z", 4, 16), ("t", 0, 1, 2), ("p", 1, 1), ("I", 2), ("c", 0), ("p", 1, 0),
-    ("p", 0, 0), ("p", 2, 0), ("p", 3, 0), ("s", 0), ("T", 1), ("sf", 1), ("I", 0), ("co", 0), ("T", 0),
-    ("sf", 2), ("cw", 4), ("zs", 4, 16), ("zs", 4, 0), ("cw", 3), ("I", 1), ("s", 1), ("co", 1), ("T", 2),
-    ("sf", 3), ("cw", 5), ("zs", 3, 32), ("zs", 3, 16), ("zs", 3, 48), ("sn", 2), ("zs", 3, 0), ("sn", 1),
-    ("cw", 2), ("co", 2), ("T", 3), ("sf", 0), ("s", 2), ("cw", 6), ("zs", 2, 32), ("sn", 3), ("zs", 2, 16),
-    ("I", 3), ("zs", 2, 48), ("zs", 2, 0), ("co", 3), ("cw", 1), ("sn", 0), ("f", 2), ("f", 1), ("cw", 7),
-    ("zs", 1, 32), ("zs", 1, 16), ("cw", 0), ("s", 3), ("zs", 1, 48), ("f", 3), ("zs", 1, 0), ("zl", 16),
-    ("zl", 32), ("zl", 0), ("zl", 48), ("tl", 1), ("tl", 0), ("s", 4),
+    "begin", ("z", 7, 0), ("z", 1, 48), ("t", 0, 1, 0), ("t", 1, 3, 0), ("z", 1, 32), ("t", 1, 1, 0),
+    ("z", 7, 16), ("z", 1, 16), ("t", 0, 3, 0), ("z", 7, 32), ("z", 1, 0), ("t", 1, 2, 0), ("z", 7, 48),
+    ("t", 0, 2, 0), ("t", 1, 0, 3), ("t", 1, 0, 1), ("z", 6, 0), ("z", 2, 48), "label", ("z", 6, 16),
+    ("t", 1, 3, 3), ("z", 2, 32), ("t", 0, 0, 3), ("t", 0, 0, 1), ("t", 0, 1, 3), ("z", 6, 32), ("z", 2, 16),
+    ("t", 0, 1, 1), ("t", 0, 3, 3), ("t", 1, 3, 1), ("z", 6, 48), ("z", 2, 0), ("z", 5, 0), ("t", 0, 3, 1),
+    ("t", 1, 1, 1), ("z", 3, 48), ("c", 3), ("t", 1, 1, 3), ("t", 1, 2, 1), ("t", 0, 2, 1), ("c", 2),
+    ("z", 5, 16), ("t", 0, 2, 3), ("z", 3, 32), ("t", 1, 2, 3), "far", ("t", 1, 2, 2), ("t", 0, 2, 2),
+    ("t", 0, 0, 2), ("t", 1, 0, 2), "labels", ("p", 0, 1), ("p", 3, 1), ("t", 1, 3, 2), ("t", 0, 1, 2),
+    ("z", 5, 32), ("z", 5, 48), ("t", 0, 3, 2), ("p", 2, 1), ("z", 4, 48), ("z", 3, 16), ("z", 3, 0),
+    ("z", 4, 0), ("z", 4, 16), ("c", 1), ("t", 1, 1, 2), ("z", 4, 32), ("p", 1, 1), ("T", 1, "a"),
+    ("T", 2, "a"), ("c", 0), ("p", 1, 0), ("p", 3, 0), ("p", 2, 0), ("p", 0, 0), ("s", 0), ("I", 0, "b"),
+    ("co", 0), ("T", 0, "b"), ("sf", 2), ("I", 1, "b"), ("cw", 4), ("zs", 4, 0), ("co", 1), ("s", 1),
+    ("zs", 4, 16), ("T", 1, "b"), ("sf", 1), ("cw", 3), ("I", 2, "a"), ("cw", 5), ("zs", 3, 32),
+    ("T", 2, "b"), ("sf", 3), ("zs", 3, 48), ("sn", 2), ("cw", 2), ("s", 2), ("zs", 3, 0), ("I", 2, "b"),
+    ("co", 2), ("zs", 3, 16), ("I", 3, "a"), ("sn", 1), ("I", 3, "b"), ("cw", 6), ("zs", 2, 32), ("co", 3),
+    ("zs", 2, 48), ("sn", 3), ("s", 3), ("zs", 2, 0), ("T", 3, "a"), ("zs", 2, 16), ("f", 2), ("cw", 7),
+    ("T", 3, "b"), ("sf", 0), ("sn", 0), ("cw", 0), ("cw", 1), ("zs", 1, 32), ("zs", 1, 48), ("s", "z"),
+    ("zs", 1, 0), ("f", 1), ("f", 3), ("zs", 1, 16), ("zl", 0), ("zl", 48), ("zl", 32), ("s", 4), ("zl", 16),
+    ("tl", 0), ("tl", 1),
 ]
 
 
@@ -106,6 +108,7 @@
     behind = {"x": device(dx=-1), "y": device(dy=-1), "z": device(dz=-1)}
     beyond = {"x": device(dx=2), "y": device(dy=2)}
     other = device(dc=1)
+    near_steps, relays = (1, -1, 2, -2), ((6, 1), (6, 2), (2, -1))
 
     own_image = pltpu.make_async_copy(
         image_hbm, image.at[pl.ds(IMAGE_AT[0, 0], ROWS)], local_sem.at[0]
@@ -125,7 +128,7 @@
     partners = [other]
     partners += [device(dx=d) for d in range(1, NX)]
     partners += [device(dy=d) for d in range(1, NY)]
-    partners += [device(dz=d) for d in range(1, NZ)]
+    partners += [device(dz=d) for d in near_steps]
     barrier = pltpu.get_barrier_semaphore()
     for partner in partners:
         pl.semaphore_signal(barrier, inc=1, device_id=partner, device_id_type=MESH)
@@ -260,14 +263,20 @@
         turned = pltpu.roll(mine, ROWS, 1)
         in_upper = jnp.broadcast_to(lax.rem(member, 2), (8, LANES)) == 1
         labels[0, 0] = jnp.where((lane >= ROWS) == in_upper, mine, turned)
-        for d in range(1, NZ):
-            there = labels.at[0, NZ - d]
+        for d in near_steps:
+            there = labels.at[0, -d % NZ]
             send("label", 1, labels.at[0, 0], there, device(dz=d), "label")
         for n in range(3):
             stats[n] = zero
 
     def on_label():
-        expect("label", labels.at[0, pl.ds(1, NZ - 1)])
+        expect("label", labels.at[0, pl.ds(0, len(near_steps))])
+        for d, step in relays:
+            here, there = labels.at[0, d], labels.at[0, (d - step) % NZ]
+            send("label", 1, here, there, device(dz=step), "far")
+
+    def on_far_label():
+        expect("far", labels.at[0, pl.ds(0, len(relays))])
         here, there = labels.at[pl.ds(0, 1)], labels.at[pl.ds(1, 1)]
         send("labels", 1, here, there, other, "labels")
 
@@ -287,6 +296,7 @@
     stretch = warmth * (1.0 / PAIRS)
     tasks["begin"] = begin
     tasks["label"] = on_label
+    tasks["far"] = on_far_label
     tasks["labels"] = on_labels
 
     def pairs(chunk, side):
@@ -339,22 +349,33 @@
             power = jnp.ceil(jnp.log2(jnp.maximum(top, SMALLEST)))
             tops[row // HALF] = jnp.broadcast_to(power, (QUARTER, LANES))
 
-    def text_part(chunk):
+    def text_part(chunk, step):
         at = pl.ds(chunk * 256, 256)
-        text_sum[at, :] = jnp.dot(
-            coef[at, :], image[...], preferred_element_type=jnp.float32
+        along = {"a": pl.ds(512, 512), "b": pl.ds(0, 512 if chunk else TILE)}[step]
+        product = jnp.dot(
+            coef[at, along], image[along, :], preferred_element_type=jnp.float32
         )
-        find_tops(text_sum, text_top, chunk * 256)
-
-    def image_part(chunk):
-        at = pl.ds(chunk * 256, 256)
-        image_sum[at, :] = lax.dot_general(
-            coef[:, at],
-            text[...],
+        if step == "b" and chunk:
+            product = product + text_sum[at, :]
+        text_sum[at, :] = product
+        if step == "b":
+            find_tops(text_sum, text_top, chunk * 256)
+
+    def image_part(part, step):
+        at = pl.ds(part * 256, 256)
+        rest = part >= 2
+        along = {"a": pl.ds(256, 768), "b": pl.ds(0, 256 if rest else TILE)}[step]
+        product = lax.dot_general(
+            coef[along, at],
+            text[along, :],
             (((0,), (0,)), ((), ())),
             preferred_element_type=jnp.float32,
         )
-        find_tops(image_sum, image_top, chunk * 256)
+        if step == "b" and rest:
+            product = product + image_sum[at, :]
+        image_sum[at, :] = product
+        if step == "b":
+            find_tops(image_sum, image_top, part * 256)
 
     messages = {}
     used = [0]
@@ -515,8 +536,11 @@
 
     for n in range(4):
         tasks["co", n] = lambda n=n: to_other(n)
-        tasks["T", n] = lambda n=n: text_part(n)
-        tasks["I", n] = lambda n=n: image_part(n)
+        for step in "ab":
+            if step == "b" or n >= 1:
+                tasks["T", n, step] = lambda a=(n, step): text_part(*a)
+            if step == "b" or n >= 2:
+                tasks["I", n, step] = lambda a=(n, step): image_part(*a)
         for chunk in range(4):
             if n < 2:
                 tasks["p", chunk, n] = lambda a=(chunk, n): pairs(*a)
@@ -539,13 +563,23 @@
         base = sum(a[0] for a in stat_axes[:nth])
         size, me, to = stat_axes[nth]
         stat_slots[base + me] = value
-        for d in range(1, size):
+        for d in near_steps if size == NZ else range(1, size):
             slot = stat_slots.at[pl.ds(base + me, 1)]
             send("stat", 1, slot, slot, to(d), ("stat", nth))
 
+    def stat_relay():
+        base = 2 + NX + NY
+        expect(("stat", 3), stat_slots.at[pl.ds(0, len(near_steps))])
+        for d, step in relays:
+            slot = stat_slots.at[pl.ds(base + lax.rem(z + d, NZ), 1)]
+            send("stat", 1, slot, slot, device(dz=step), ("stat", 4))
+
     def stat_sum(nth):
         base, size = sum(a[0] for a in stat_axes[:nth]), stat_axes[nth][0]
-        expect(("stat", nth), stat_slots.at[pl.ds(0, size - 1)])
+        if size == NZ:
+            expect(("stat", 4), stat_slots.at[pl.ds(0, len(relays))])
+        else:
+            expect(("stat", nth), stat_slots.at[pl.ds(0, size - 1)])
         value = stat_slots[base]
         for n in range(1, size):
             value = value + stat_slots[base + n]
@@ -566,6 +600,7 @@
     tasks["s", 0] = first_stats
     for n in (1, 2, 3):
         tasks["s", n] = lambda n=n: stat_send(n, stat_sum(n - 1))
+    tasks["s", "z"] = stat_relay
     tasks["s", 4] = last_stats
 
     for task in ORDER:
@@ -587,9 +622,10 @@
     smem = pl.BlockSpec(memory_space=pltpu.SMEM)
     hbm = pl.BlockSpec(memory_space=pl.ANY)
     grad = pltpu.VMEM((ROWS, D), jnp.float32)
+    sums = jax.ShapeDtypeStruct((3,), jnp.float32)
     return pl.pallas_call(
         kernel,
-        out_shape=(grad, grad, jax.ShapeDtypeStruct((3,), jnp.float32)),
+        out_shape=(grad, grad, sums),
         in_specs=[hbm, hbm, vmem, hbm, hbm],
         out_specs=(vmem, vmem, smem),
         scratch_shapes=[

time: 59.5 us -> 58.6 us (0.985)
  Pallas kernels: 55.5 us -> 54.6 us
    pallas_call x1, Pallas kernels: 55.5 us -> 54.6 us  [on_device(): pl.pallas_call(kernel, out_shape=(grad, grad, sums), in_specs=[hbm, hbm,...]
where the time goes in v4:
time: 58.6 us; the launch traced here: 58.5 us
  Pallas kernels  54.6 us (93%)
  local copies, waits for them, and re-layouts  1.94 us (3%)
  between operations  1.93 us (3%)
    pallas_call x1, Pallas kernels, on_device(): pl.pallas_call(kernel, out_shape=(grad, grad, sums), in_specs=[hbm, hbm,...  54.6 us
    unnamed x5, local copies, waits for them, and re-layouts  1.94 us

profile of v4, /device:TPU:1, one launch (start us, length us, event | category | flops | bytes accessed | tf_op | source)
XLA Modules:
  0.0 58.5 jit_solution(17865318412926542869)
XLA Ops:
  1.9 54.6 %shard_map.76 = (f32[64,1152]{1,0:T(8,128)S(1)}, f32[64,1152]{1,0:T(8,128)S(1)}, f32[3]{0:T(128)}) custom-call(f32[1]{0:T(128)S(6)} %copy.13.warmth_hbm, f32[1]{0:T(128)S(6)} %copy.14.offset_hbm, s32[4,128]{1,0:T(4,128)} %bitcast.1, bf16[64,1152]{1,0:T(8,128)(2,1)} %image_hbm.1, bf16[64,1152]{1,0:T(8,128)(2,1)} %text_hbm.1), custom_call_target="tpu_custom_call" | custom-call | tf_op jit(solution)/shard_map/pallas_call | solution.py:626
  56.5 0.7 %copy.11 = f32[64,1152]{1,0:T(8,128)} copy(f32[64,1152]{1,0:T(8,128)S(1)} %get-tuple-element.3) | data formatting | bytes 589824
  57.2 0.0 copy-start
  57.2 0.7 %copy.12 = f32[64,1152]{1,0:T(8,128)} copy(f32[64,1152]{1,0:T(8,128)S(1)} %get-tuple-element.4) | data formatting | bytes 589824
  57.9 0.0 copy-done
  58.0 0.5 copy.15
Async XLA Ops:
  57.2 0.7 %copy-start = (f32[3]{0:T(128)S(1)}, f32[3]{0:T(128)}, u32[]{:S(2)}) copy-start(f32[3]{0:T(128)} %get-tuple-element.11) | copy-start | bytes 40

commit v5 on v4

--- a/solution.py
+++ b/solution.py
@@ -32,24 +32,23 @@
 N_TILES = 1152
 ORDER = [
     "begin", ("z", 7, 0), ("z", 1, 48), ("t", 0, 1, 0), ("t", 1, 3, 0), ("z", 1, 32), ("t", 1, 1, 0),
-    ("z", 7, 16), ("z", 1, 16), ("t", 0, 3, 0), ("z", 7, 32), ("z", 1, 0), ("t", 1, 2, 0), ("z", 7, 48),
-    ("t", 0, 2, 0), ("t", 1, 0, 3), ("t", 1, 0, 1), ("z", 6, 0), ("z", 2, 48), "label", ("z", 6, 16),
-    ("t", 1, 3, 3), ("z", 2, 32), ("t", 0, 0, 3), ("t", 0, 0, 1), ("t", 0, 1, 3), ("z", 6, 32), ("z", 2, 16),
-    ("t", 0, 1, 1), ("t", 0, 3, 3), ("t", 1, 3, 1), ("z", 6, 48), ("z", 2, 0), ("z", 5, 0), ("t", 0, 3, 1),
-    ("t", 1, 1, 1), ("z", 3, 48), ("c", 3), ("t", 1, 1, 3), ("t", 1, 2, 1), ("t", 0, 2, 1), ("c", 2),
-    ("z", 5, 16), ("t", 0, 2, 3), ("z", 3, 32), ("t", 1, 2, 3), "far", ("t", 1, 2, 2), ("t", 0, 2, 2),
+    ("z", 7, 16), ("z", 1, 16), ("t", 0, 3, 0), ("z", 7, 32), ("z", 7, 48), ("z", 1, 0), ("t", 1, 2, 0),
+    ("t", 0, 2, 0), "label", ("t", 1, 0, 3), ("z", 6, 0), ("z", 2, 48), ("t", 1, 0, 1), ("z", 6, 16),
+    ("t", 1, 3, 3), ("z", 2, 32), ("t", 0, 0, 3), ("c", 3), ("t", 0, 0, 1), ("t", 0, 1, 3), ("z", 6, 32),
+    ("t", 1, 1, 3), ("z", 2, 16), ("t", 0, 1, 1), ("t", 1, 3, 1), ("z", 6, 48), ("z", 2, 0), ("t", 0, 3, 3),
+    ("z", 5, 0), ("t", 1, 1, 1), ("t", 0, 3, 1), ("z", 3, 48), ("t", 1, 2, 1), "far", ("t", 0, 2, 1),
+    ("z", 5, 16), ("c", 2), ("t", 0, 2, 3), ("z", 3, 32), ("t", 1, 2, 3), ("t", 1, 2, 2), ("t", 0, 2, 2),
     ("t", 0, 0, 2), ("t", 1, 0, 2), "labels", ("p", 0, 1), ("p", 3, 1), ("t", 1, 3, 2), ("t", 0, 1, 2),
-    ("z", 5, 32), ("z", 5, 48), ("t", 0, 3, 2), ("p", 2, 1), ("z", 4, 48), ("z", 3, 16), ("z", 3, 0),
-    ("z", 4, 0), ("z", 4, 16), ("c", 1), ("t", 1, 1, 2), ("z", 4, 32), ("p", 1, 1), ("T", 1, "a"),
-    ("T", 2, "a"), ("c", 0), ("p", 1, 0), ("p", 3, 0), ("p", 2, 0), ("p", 0, 0), ("s", 0), ("I", 0, "b"),
-    ("co", 0), ("T", 0, "b"), ("sf", 2), ("I", 1, "b"), ("cw", 4), ("zs", 4, 0), ("co", 1), ("s", 1),
-    ("zs", 4, 16), ("T", 1, "b"), ("sf", 1), ("cw", 3), ("I", 2, "a"), ("cw", 5), ("zs", 3, 32),
-    ("T", 2, "b"), ("sf", 3), ("zs", 3, 48), ("sn", 2), ("cw", 2), ("s", 2), ("zs", 3, 0), ("I", 2, "b"),
-    ("co", 2), ("zs", 3, 16), ("I", 3, "a"), ("sn", 1), ("I", 3, "b"), ("cw", 6), ("zs", 2, 32), ("co", 3),
-    ("zs", 2, 48), ("sn", 3), ("s", 3), ("zs", 2, 0), ("T", 3, "a"), ("zs", 2, 16), ("f", 2), ("cw", 7),
-    ("T", 3, "b"), ("sf", 0), ("sn", 0), ("cw", 0), ("cw", 1), ("zs", 1, 32), ("zs", 1, 48), ("s", "z"),
-    ("zs", 1, 0), ("f", 1), ("f", 3), ("zs", 1, 16), ("zl", 0), ("zl", 48), ("zl", 32), ("s", 4), ("zl", 16),
-    ("tl", 0), ("tl", 1),
+    ("z", 3, 16), ("z", 5, 32), ("z", 5, 48), ("t", 0, 3, 2), ("z", 3, 0), ("p", 2, 1), ("z", 4, 0),
+    ("z", 4, 16), ("z", 4, 48), ("z", 4, 32), ("t", 1, 1, 2), ("c", 1), ("p", 1, 1), ("T", 1, "a"), ("c", 0),
+    ("p", 1, 0), ("p", 3, 0), ("p", 2, 0), ("p", 0, 0), ("s", 0), ("T", 0, "b"), ("I", 0, "b"), ("co", 0),
+    ("T", 2, "a"), ("I", 1, "b"), ("cw", 4), ("sf", 2), ("zs", 4, 0), ("zs", 4, 16), ("co", 1), ("I", 2, "a"),
+    ("cw", 3), ("s", 1), ("T", 1, "b"), ("cw", 5), ("zs", 3, 32), ("zs", 3, 48), ("sf", 1), ("T", 2, "b"),
+    ("sf", 3), ("zs", 3, 0), ("sn", 2), ("I", 2, "b"), ("s", 2), ("co", 2), ("zs", 3, 16), ("I", 3, "a"),
+    ("cw", 2), ("sn", 1), ("cw", 6), ("zs", 2, 32), ("zs", 2, 48), ("sn", 3), ("I", 3, "b"), ("co", 3),
+    ("zs", 2, 0), ("f", 2), ("s", 3), ("zs", 2, 16), ("T", 3, "a"), ("T", 3, "b"), ("sf", 0), ("sn", 0),
+    ("cw", 0), ("cw", 7), ("cw", 1), ("zs", 1, 48), ("zs", 1, 0), ("f", 1), ("zs", 1, 32), ("f", 3),
+    ("s", "z"), ("zs", 1, 16), ("zl", 0), ("zl", 48), ("tl", 0), ("s", 4), ("zl", 32), ("zl", 16), ("tl", 1),
 ]
 
 

time: 58.6 us -> 59.1 us (level)
  no operation moved by 1% of the time
where the time goes in v5:
time: 59.1 us; the launch traced here: 59 us
  Pallas kernels  55.1 us (93%)
  local copies, waits for them, and re-layouts  1.94 us (3%)
  between operations  1.93 us (3%)
    pallas_call x1, Pallas kernels, on_device(): pl.pallas_call(kernel, out_shape=(grad, grad, sums), in_specs=[hbm, hbm,...  55.1 us
    unnamed x5, local copies, waits for them, and re-layouts  1.94 us

profile of v5, /device:TPU:1, one launch (start us, length us, event | category | flops | bytes accessed | tf_op | source)
XLA Modules:
  0.0 59.0 jit_solution(16613270281705730401)
XLA Ops:
  1.9 55.1 %shard_map.76 = (f32[64,1152]{1,0:T(8,128)S(1)}, f32[64,1152]{1,0:T(8,128)S(1)}, f32[3]{0:T(128)}) custom-call(f32[1]{0:T(128)S(6)} %copy.13.warmth_hbm, f32[1]{0:T(128)S(6)} %copy.14.offset_hbm, s32[4,128]{1,0:T(4,128)} %bitcast.1, bf16[64,1152]{1,0:T(8,128)(2,1)} %image_hbm.1, bf16[64,1152]{1,0:T(8,128)(2,1)} %text_hbm.1), custom_call_target="tpu_custom_call" | custom-call | tf_op jit(solution)/shard_map/pallas_call | solution.py:625
  57.0 0.7 %copy.11 = f32[64,1152]{1,0:T(8,128)} copy(f32[64,1152]{1,0:T(8,128)S(1)} %get-tuple-element.3) | data formatting | bytes 589824
  57.7 0.0 copy-start
  57.7 0.7 %copy.12 = f32[64,1152]{1,0:T(8,128)} copy(f32[64,1152]{1,0:T(8,128)S(1)} %get-tuple-element.4) | data formatting | bytes 589824
  58.4 0.0 copy-done
  58.4 0.5 copy.15
Async XLA Ops:
  57.7 0.7 %copy-start = (f32[3]{0:T(128)S(1)}, f32[3]{0:T(128)}, u32[]{:S(2)}) copy-start(f32[3]{0:T(128)} %get-tuple-element.11) | copy-start | bytes 40
